TPU v7x, 256 devices: a whole 4x4x8 slice. The times are simulated.
256 devices in a mesh: tm: 64 (over x, z, core), heads: 4 (over y).
Axes of the slice: x: 4, y: 4, z: 8, core: 2. Of those that a mesh axis runs over, the one named last changes fastest.
Arguments:
- slab_tokens: bfloat16 [32768, 3584], P('tm', 'heads'), may hold values from -14 to 14
- memory: bfloat16 [32768, 3584], P('tm', 'heads'), may hold values from -14 to 14
- query_weight: bfloat16 [3584, 3584], P(None, 'heads'), may hold values from -0.09375 to 0.09375
- key_weight: bfloat16 [3584, 512], P(None, 'heads'), may hold values from -0.09375 to 0.09375
- value_weight: bfloat16 [3584, 512], P(None, 'heads'), may hold values from -0.09375 to 0.09375
- query_down: bfloat16 [16, 3584], replicated, may hold values from -0.09375 to 0.09375
- query_up: bfloat16 [16, 3584], P(None, 'heads'), may hold values from -1.5 to 1.5
- value_down: bfloat16 [16, 3584], replicated, may hold values from -0.09375 to 0.09375
- value_up: bfloat16 [16, 512], P(None, 'heads'), may hold values from -1.5 to 1.5
- tag_weight: bfloat16 [3584, 8], P('heads'), may hold values from -0.75 to 0.75
- retrieval: int32 [256, 8], P('tm'), may hold values from 0 to 255, as said below
- boundary: int32 [256], P('tm'), may hold values from 0 to 127
- grad_tags: float32 [32768, 8], P('tm'), may hold values from -0.125 to 0.125
Outputs:
- tag_logits: float32 [32768, 8], P('tm')
- query_down_grad: float32 [16, 3584], P(None, 'heads')
- query_up_grad: float32 [16, 3584], P(None, 'heads')
- value_down_grad: float32 [16, 3584], P(None, 'heads')
- value_up_grad: float32 [16, 512], P(None, 'heads')
Inputs may be any that keep to these rules, and one draw needn't show every extreme that they name: `retrieval`: each row names 8 different memory blocks; the rows of one index of tm name at most 1 different blocks held by any one index of tm.
All inputs are finite; a program needn't handle non-finite values.
Results may differ from a plain program's by a relative error of at most 0.035.
The roundings to bfloat16 on the way count: a program that leaves them out, or rounds other values in their place, can miss the bound.
Values may be sent and summed in bfloat16 or wider, within the bound.
A program may use at most 128 MiB of HBM per device.

v0:
```python
import jax
import jax.numpy as jnp
from jax import lax
from jax.sharding import PartitionSpec as P

HD = 128
RANK = 16
TOP = 8
BLK = 128
CAP = 1


HIGHEST = lax.Precision.HIGHEST


def attend(query, all_keys, all_values, split_row, out_grad):
    span_count, row_count, query_width = query.shape
    key_count, kv_width = (all_keys.shape[1], all_keys.shape[2])
    kv_heads = kv_width // HD
    group_size = query_width // kv_width
    score_scale = HD ** (-0.5)
    query_heads = query.reshape(span_count, row_count, kv_heads, group_size, HD)
    key_heads = all_keys.reshape(span_count, key_count, kv_heads, HD)
    value_heads = all_values.reshape(span_count, key_count, kv_heads, HD)
    grad_heads = out_grad.reshape(span_count, row_count, kv_heads, group_size, HD)
    scores = (
        jnp.einsum("crngd,cknd->cngrk", query_heads, key_heads, preferred_element_type=jnp.float32)
        * score_scale
    )
    row_ids = jnp.arange(row_count, dtype=jnp.int32)[:, None]
    col_ids = jnp.arange(BLK, dtype=jnp.int32)[None, :]
    edge_at = split_row[:, None, None]
    local_seen = (col_ids <= row_ids) & ((col_ids >= edge_at) | (row_ids < edge_at))
    visible = jnp.concatenate(
        [jnp.ones((span_count, row_count, key_count - BLK), jnp.bool_), local_seen], axis=2
    )
    scores = jnp.where(visible[:, None, None], scores, -jnp.inf)
    row_max = jnp.max(scores, axis=-1, keepdims=True)
    weights = jnp.exp(scores - row_max)
    probs = weights / jnp.sum(weights, axis=-1, keepdims=True)
    probs_low = probs.astype(jnp.bfloat16)
    attended = jnp.einsum(
        "cngrk,cknd->crngd", probs_low, value_heads, preferred_element_type=jnp.float32
    ).astype(jnp.bfloat16)
    prob_grad = jnp.einsum(
        "crngd,cknd->cngrk", grad_heads, value_heads, preferred_element_type=jnp.float32
    )
    row_dot = jnp.sum(grad_heads.astype(jnp.float32) * attended.astype(jnp.float32), axis=-1)
    row_dot = jnp.transpose(row_dot, (0, 2, 3, 1))[..., None]
    score_grad = (probs * (prob_grad - row_dot) * score_scale).astype(jnp.bfloat16)
    query_grad = jnp.einsum(
        "cngrk,cknd->crngd", score_grad, key_heads, preferred_element_type=jnp.float32
    ).astype(jnp.bfloat16)
    value_grad = jnp.einsum(
        "cngrk,crngd->cknd", probs_low, grad_heads, preferred_element_type=jnp.float32
    )
    return (
        attended.reshape(span_count, row_count, query_width),
        query_grad.reshape(span_count, row_count, query_width),
        value_grad.reshape(span_count, key_count, kv_width),
    )


def choose_slots(needed, places):
    slot_ids = jnp.arange(CAP, dtype=jnp.int32)
    return needed[:, None, :] * (places[:, None, :] == slot_ids[None, :, None]).astype(jnp.int32)


def local(
    slab_tokens,
    memory,
    query_weight,
    key_weight,
    value_weight,
    query_down,
    query_up,
    value_down,
    value_up,
    tag_weight,
    retrieval,
    boundary,
    grad_tags,
):
    tok_rows = slab_tokens.shape[0]
    mem_rows = memory.shape[0]
    query_width = query_weight.shape[1]
    kv_width = key_weight.shape[1]
    span_count = tok_rows // BLK
    block_count = mem_rows // BLK
    pair_weight = jnp.concatenate([key_weight, value_weight], 1)
    adapter_pair = jnp.concatenate([query_down, value_down], 0)
    contract_last = (((1,), (1,)), ((), ()))
    contract_first = (((0,), (0,)), ((), ()))
    token_piece = lax.all_gather(slab_tokens, "heads", axis=1, tiled=True)
    memory_piece = lax.all_gather(memory, "heads", axis=1, tiled=True)
    query_acc = jnp.dot(token_piece, query_weight, preferred_element_type=jnp.float32)
    pair_acc = jnp.dot(token_piece, pair_weight, preferred_element_type=jnp.float32)
    low_acc = lax.dot_general(
        token_piece, adapter_pair, contract_last, preferred_element_type=jnp.float32
    )
    memory_acc = jnp.dot(memory_piece, pair_weight, preferred_element_type=jnp.float32)
    memory_low_acc = lax.dot_general(
        memory_piece, adapter_pair[RANK:], contract_last, preferred_element_type=jnp.float32
    )
    query_acc, pair_acc, low_acc, memory_acc, memory_low_acc = (
        query_acc,
        pair_acc,
        low_acc,
        memory_acc,
        memory_low_acc,
    )
    low_tokens = low_acc.astype(jnp.bfloat16)
    low_query = low_tokens[:, :RANK]
    low_value = low_tokens[:, RANK:]
    queries = (query_acc + jnp.dot(low_query, query_up, preferred_element_type=jnp.float32)).astype(
        jnp.bfloat16
    )
    keys_local = pair_acc[:, :kv_width].astype(jnp.bfloat16)
    values_local = (
        pair_acc[:, kv_width:] + jnp.dot(low_value, value_up, preferred_element_type=jnp.float32)
    ).astype(jnp.bfloat16)
    memory_low = memory_low_acc.astype(jnp.bfloat16)
    memory_pair = (
        jnp.concatenate(
            [
                memory_acc[:, :kv_width],
                memory_acc[:, kv_width:]
                + jnp.dot(memory_low, value_up, preferred_element_type=jnp.float32),
            ],
            1,
        )
        .astype(jnp.bfloat16)
        .reshape(block_count, BLK, 2 * kv_width)
    )
    peer_count = lax.axis_size("tm")
    every_block = jnp.arange(peer_count * block_count, dtype=jnp.int32)
    wanted = (
        jnp.any(retrieval.reshape(-1, 1) == every_block[None, :], axis=0)
        .astype(jnp.int32)
        .reshape(peer_count, block_count)
    )
    places = jnp.cumsum(wanted, axis=1) - wanted
    requested = choose_slots(wanted, places)
    asked_for = lax.all_to_all(requested, "tm", split_axis=0, concat_axis=0, tiled=True)
    rows_needed = retrieval // block_count * CAP + jnp.take(places.reshape(-1), retrieval)
    asked_low = asked_for.astype(jnp.bfloat16)
    outgoing = jnp.einsum(
        "rcm,mbw->rcbw", asked_low, memory_pair, preferred_element_type=jnp.float32
    ).astype(jnp.bfloat16)
    fetched = lax.all_to_all(outgoing, "tm", split_axis=0, concat_axis=0, tiled=True)
    slot_rows = fetched.reshape(peer_count * CAP, BLK, 2 * kv_width)
    picked = jnp.take(slot_rows, rows_needed.reshape(-1), axis=0).reshape(
        span_count, TOP * BLK, 2 * kv_width
    )
    all_keys = jnp.concatenate(
        [picked[..., :kv_width], keys_local.reshape(span_count, BLK, kv_width)], 1
    )
    all_values = jnp.concatenate(
        [picked[..., kv_width:], values_local.reshape(span_count, BLK, kv_width)], 1
    )
    attended_grad = lax.dot_general(
        grad_tags, tag_weight.astype(jnp.float32), contract_last, precision=HIGHEST
    ).astype(jnp.bfloat16)
    attended, query_grad, value_grad = attend(
        queries.reshape(span_count, BLK, query_width),
        all_keys,
        all_values,
        boundary,
        attended_grad.reshape(span_count, BLK, query_width),
    )
    attended = attended.reshape(tok_rows, query_width)
    query_grad = query_grad.reshape(tok_rows, query_width)
    logits_out = lax.psum(
        jnp.dot(attended, tag_weight, preferred_element_type=jnp.float32), "heads"
    )
    local_grad = value_grad[:, TOP * BLK :].reshape(tok_rows, kv_width)
    slot_grads = value_grad[:, : TOP * BLK].reshape(span_count * TOP, BLK * kv_width)
    slot_hits = (
        rows_needed.reshape(-1, 1) == jnp.arange(peer_count * CAP, dtype=jnp.int32)[None, :]
    ).astype(jnp.float32)
    grad_buffer = lax.dot_general(slot_hits, slot_grads, contract_first, precision=HIGHEST).reshape(
        peer_count * CAP, BLK, kv_width
    )
    up_wide = value_up.astype(jnp.float32)
    returned = lax.all_to_all(
        grad_buffer.reshape(peer_count, CAP, BLK, kv_width),
        "tm",
        split_axis=0,
        concat_axis=0,
        tiled=True,
    )
    owned_grad = jnp.einsum(
        "rcm,rcbw->mbw", asked_for.astype(jnp.float32), returned, precision=HIGHEST
    ).reshape(mem_rows, kv_width)
    memory_cot = lax.dot_general(up_wide, owned_grad, contract_last, precision=HIGHEST)
    up_memory = lax.dot_general(
        memory_low.astype(jnp.float32), owned_grad, contract_first, precision=HIGHEST
    )
    query_cot = lax.dot_general(
        query_up, query_grad, contract_last, preferred_element_type=jnp.float32
    )
    value_cot = lax.dot_general(up_wide, local_grad, contract_last, precision=HIGHEST)
    query_cot, value_cot, memory_cot = lax.psum((query_cot, value_cot, memory_cot), "heads")
    query_down_grad = jnp.dot(
        query_cot.astype(jnp.bfloat16), slab_tokens, preferred_element_type=jnp.float32
    )
    value_down_grad = jnp.dot(
        value_cot.astype(jnp.bfloat16), slab_tokens, preferred_element_type=jnp.float32
    ) + jnp.dot(memory_cot.astype(jnp.bfloat16), memory, preferred_element_type=jnp.float32)
    query_up_grad = lax.dot_general(
        low_query, query_grad, contract_first, preferred_element_type=jnp.float32
    )
    value_up_grad = (
        lax.dot_general(
            low_value.astype(jnp.float32), local_grad, contract_first, precision=HIGHEST
        )
        + up_memory
    )
    query_down_grad, query_up_grad, value_down_grad, value_up_grad = lax.psum(
        (query_down_grad, query_up_grad, value_down_grad, value_up_grad), "tm"
    )
    return (logits_out, query_down_grad, query_up_grad, value_down_grad, value_up_grad)


def solution(mesh):
    in_specs = (
        P("tm", "heads"),
        P("tm", "heads"),
        P(None, "heads"),
        P(None, "heads"),
        P(None, "heads"),
        P(),
        P(None, "heads"),
        P(),
        P(None, "heads"),
        P("heads", None),
        P("tm", None),
        P("tm"),
        P("tm", None),
    )
    out_specs = (
        P("tm", None),
        P(None, "heads"),
        P(None, "heads"),
        P(None, "heads"),
        P(None, "heads"),
    )
    return jax.shard_map(local, mesh=mesh, in_specs=in_specs, out_specs=out_specs, check_vma=False)
```

profile of v0, /device:TPU:1, one launch (start us, length us, event | category | flops | bytes accessed | tf_op | source)
XLA Modules:
  0.0 533.5 jit_solution(7502799912866734459)
XLA Ops:
  9.8 13.0 %all-to-all-start = ((s32[64,1,4]{2,1,0:T(1,128)}), s32[64,1,4]{2,1,0:T(1,128)S(1)}, u32[]{:S(2)}, u32[]{:S(2)}) async-start(s32[64,1,4]{2,1,0:T(1,128)} %bitcast.1), calls=%async_computation | async-start | bytes 65536 | tf_op jit(solution)/shard_map/all_to_all | solution.py:144
  24.4 7.6 %all-to-all-done = s32[64,1,4]{2,1,0:T(1,128)S(1)} async-done(((s32[64,1,4]{2,1,0:T(1,128)}), s32[64,1,4]{2,1,0:T(1,128)S(1)}, u32[]{:S(2)}, u32[]{:S(2)}) %all-to-all-start) | async-done | bytes 1056 | tf_op jit(solution)/shard_map/all_to_all | solution.py:144
  32.1 28.1 %all-gather.3.cloned.1.call-done = bf16[512,3584]{1,0:T(8,128)(2,1)} async-done(((bf16[512,896]{1,0:T(8,128)(2,1)}), bf16[512,3584]{1,0:T(8,128)(2,1)}) %all-gather.3.cloned.1.call-update) | async-done | bytes 3670032 | tf_op jit(solution)/shard_map/all_gather | solution.py:95
  60.1 3.2 convolution_bitcast_fusion.2
  63.6 3.1 convolution_convert_fusion.2
  68.4 4.4 copy.96
  72.9 11.0 %all-to-all-start.1 = ((bf16[64,1,128,256]{3,2,1,0:T(8,128)(2,1)}), bf16[64,1,128,256]{3,2,1,0:T(8,128)(2,1)}, u32[]{:S(2)}, u32[]{:S(2)}) async-start(bf16[64,1,128,256]{3,2,1,0:T(8,128)(2,1)} %copy.96), calls=%async_computation.1 | async-start | bytes 8388608 | tf_op jit(solution)/shard_map/all_to_all | solution.py:150
  88.0 1.7 copy.112
  90.8 42.1 %all-gather.5.cloned.1.call-done = bf16[512,3584]{1,0:T(8,128)(2,1)} async-done(((bf16[512,896]{1,0:T(8,128)(2,1)}), bf16[512,3584]{1,0:T(8,128)(2,1)}) %all-gather.5.cloned.1.call-update) | async-done | bytes 3670032 | tf_op jit(solution)/shard_map/all_gather | solution.py:94
  133.0 3.3 fusion.31
  136.4 7.6 %fusion.83 = f32[512,896]{1,0:T(8,128)S(1)} fusion(bf16[512,3584]{1,0:T(8,128)(2,1)S(1)} %copy-done.3, bf16[3584,896]{1,0:T(8,128)(2,1)} %param.15), kind=kOutput, calls=%fused_computation.122 | convolution fusion | flops 3288334336 | bytes 11927552 | tf_op jit(solution)/shard_map/dot_general | solution.py:96
  144.4 2.0 reshape.312
  146.4 3.7 convolution_bitcast_fusion.1
  150.3 29.4 %all-to-all-done.1 = bf16[64,1,128,256]{3,2,1,0:T(8,128)(2,1)} async-done(((bf16[64,1,128,256]{3,2,1,0:T(8,128)(2,1)}), bf16[64,1,128,256]{3,2,1,0:T(8,128)(2,1)}, u32[]{:S(2)}, u32[]{:S(2)}) %all-to-all-start.1) | async-done | bytes 4194336 | tf_op jit(solution)/shard_map/all_to_all | solution.py:150
  179.8 2.9 gather_fusion.1
  185.2 7.0 %fusion.3 = (f32[4,7,128]{2,1,0:T(8,128)S(1)}, f32[4,1152,128,7]{2,1,3,0:T(8,128)}) fusion(pred[4,128,1152]{1,2,0:T(8,128)(4,1)S(1)} %copy-done.4, bf16[4,128,7,128]{3,2,1,0:T(8,128)(2,1)S(1)} %copy-done.8, bf16[4,128,128]{2,1,0:T(8,128)(2,1)S(1)} %bitcast.233, bf16[4,1024,128]{2,1,0:T(8,128)(2,1)S(1)} %get-tuple-element.15), kind=kOutput, calls=%fused_computation.9 | convolution fusion | flops 1071706624 | bytes 19216384 | tf_op jit(solution)/shard_map/crngd,cknd->cngrk/dot_general | solution.py:27
  192.2 8.8 %fusion.5 = f32[4,7,128]{2,1,0:T(8,128)S(1)} fusion(f32[4,1152,128,7]{2,1,3,0:T(8,128)} %get-tuple-element.20, f32[4,7,128]{2,1,0:T(8,128)S(1)} %get-tuple-element.19, pred[4,128,1152]{1,2,0:T(8,128)(4,1)S(1)} %copy-done.5), kind=kLoop, calls=%fused_computation.11 | loop fusion | flops 12382720 | bytes 17133568 | tf_op jit(solution)/shard_map/reduce_sum | solution.py:40
  201.0 8.4 %fusion.15 = f32[4,1152,128]{1,2,0:T(8,128)S(1)} fusion(bf16[4,128,7,128]{1,3,2,0:T(8,128)(2,1)S(1)} %copy-done.13, f32[4,7,128]{2,1,0:T(8,128)S(1)} %fusion.5, f32[4,7,128]{2,1,0:T(8,128)S(1)} %get-tuple-element.19, f32[4,1152,128,7]{2,1,3,0:T(8,128)} %get-tuple-element.20, pred[4,128,1152]{1,2,0:T(8,128)(4,1)S(1)} %copy-done.5), kind=kOutput, calls=%fused_computation.22 | convolution fusion | flops 1073479680 | bytes 20410368 | tf_op jit(solution)/shard_map/cngrk,crngd->cknd/dot_general | solution.py:54
  209.4 1.5 copy-done.7
  211.2 1.8 copy.116
  213.0 1.7 reshape.279
  214.8 2.0 convolution_bitcast_fusion
  216.7 4.4 copy.118
  221.1 5.9 %all-to-all-start.2 = ((f32[64,1,128,128]{3,2,1,0:T(8,128)}), f32[64,1,128,128]{3,2,1,0:T(8,128)}, u32[]{:S(2)}, u32[]{:S(2)}) async-start(f32[64,1,128,128]{3,2,1,0:T(8,128)} %copy.118), calls=%async_computation.2 | async-start | bytes 8388608 | tf_op jit(solution)/shard_map/all_to_all | solution.py:185
  228.1 1.9 copy.108
  231.3 11.8 %multiply_reduce_fusion = (f32[4,128,7]{1,2,0:T(8,128)S(1)}, bf16[4,128,1,7,128]{1,4,3,0,2:T(8,128)(2,1)}) fusion(f32[4,128,1,7,128]{1,4,3,0,2:T(8,128)} %copy.108, f32[4,7,128]{2,1,0:T(8,128)S(1)} %fusion.5, f32[4,7,128]{2,1,0:T(8,128)S(1)} %get-tuple-element.19, f32[4,1152,128,7]{2,1,3,0:T(8,128)} %get-tuple-element.20, ...), kind=kOutput, calls=%fused_computation.28 | convolution fusion | flops 1077670400 | bytes 21080064 | tf_op jit(solution)/shard_map/cngrk,cknd->crngd/dot_general | solution.py:42
  243.1 11.2 %fusion.25 = bf16[4,128,1,7,128]{1,4,3,0,2:T(8,128)(2,1)} fusion(bf16[4,128,7,128]{1,3,2,0:T(8,128)(2,1)} %copy.112, f32[4,7,128]{2,1,0:T(8,128)S(1)} %bitcast.238, f32[4,7,128]{2,1,0:T(8,128)S(1)} %fusion.5, f32[4,7,128]{2,1,0:T(8,128)S(1)} %get-tuple-element.19, f32[4,1152,128,7]{2,1,3,0:T(8,128)} %get-tuple-element.20, ...), kind=kOutput, calls=%fused_computation.33 | convolution fusion | flops 2148007936 | bytes 21342208 | tf_op jit(solution)/shard_map/cngrk,cknd->crngd/dot_general | solution.py:51
  254.3 2.0 copy.111
  259.1 63.8 %all-to-all-done.2 = f32[64,1,128,128]{3,2,1,0:T(8,128)} async-done(((f32[64,1,128,128]{3,2,1,0:T(8,128)}), f32[64,1,128,128]{3,2,1,0:T(8,128)}, u32[]{:S(2)}, u32[]{:S(2)}) %all-to-all-start.2) | async-done | bytes 4194336 | tf_op jit(solution)/shard_map/all_to_all | solution.py:185
  323.0 6.4 %fusion.12 = f32[4,128,128]{2,0,1:T(4,128)S(1)} fusion(f32[64,1,128,128]{3,2,1,0:T(8,128)} %all-to-all-done.2, s32[64,1,4]{0,2,1:T(4,128)S(1)} %copy.92), kind=kOutput, calls=%fused_computation.18 | convolution fusion | flops 50331904 | bytes 4457472 | tf_op jit(solution)/shard_map/rcm,rcbw->mbw/dot_general | solution.py:192
  330.5 13.2 %all-reduce.7 = (f32[512,8]{0,1:T(8,128)}, bf16[16,512]{1,0:T(8,128)(2,1)S(1)}, bf16[16,512]{1,0:T(8,128)(2,1)S(1)}, bf16[16,512]{1,0:T(8,128)(2,1)S(1)}) all-reduce(f32[512,8]{0,1:T(8,128)S(1)} %fusion.35, f32[16,512]{1,0:T(8,128)S(1)} %convolution_bitcast_fusion.3, ...), channel_id=1, replica_groups=mesh['tm'=64,'heads'=4] {'heads'}, use_global_device_ids=true, to_apply=%region_4.5 | all-reduce | flops 28672 | bytes 180224 | tf_op jit(solution)/shard_map/psum | solution.py:173
  345.7 175.4 %all-reduce.6.cloned.1.call-done = (f32[16,896]{1,0:T(8,128)}, f32[16,896]{1,0:T(8,128)}, f32[16,896]{1,0:T(8,128)}, f32[16,128]{1,0:T(8,128)}) async-done(((f32[16,896]{1,0:T(8,128)}, f32[16,896]{1,0:T(8,128)}, f32[16,896]{1,0:T(8,128)}, f32[16,128]{1,0:T(8,128)}), (f32[16,896]{1,0:T(8,128)}, f32[16,896]{1,0:T(8,128)}, f32[16,896]{1,0:T(8,128)}, f32[16,128]{1,0:T(8,128)})) %all-reduce.6.cloned.1.call-update) | async-done | bytes 180240 | tf_op jit(solution)/shard_map/psum | solution.py:219
  (116 shorter events, 28.5 us)
Async XLA Ops:
  7.2 136.8 %copy-start = (bf16[16,896]{1,0:T(8,128)(2,1)S(1)}, bf16[16,896]{1,0:T(8,128)(2,1)}, u32[]{:S(2)}) copy-start(bf16[16,896]{1,0:T(8,128)(2,1)} %param.19) | copy-start | bytes 86020
  7.2 17.0 %copy-start.11 = (bf16[3584,128]{1,0:T(8,128)(2,1)S(1)}, bf16[3584,128]{1,0:T(8,128)(2,1)}, u32[]{:S(2)}) copy-start(bf16[3584,128]{1,0:T(8,128)(2,1)} %param.17) | copy-start | bytes 2752516
  7.2 53.0 %all-gather.3.cloned.1.call-start = ((), (), s32[]{:S(2)}) async-start(), calls=%async_computation.3 | async-start | bytes 4587520 | tf_op jit(solution)/shard_map/all_gather | solution.py:95
  9.8 22.2 %all-to-all-start = ((s32[64,1,4]{2,1,0:T(1,128)}), s32[64,1,4]{2,1,0:T(1,128)S(1)}, u32[]{:S(2)}, u32[]{:S(2)}) async-start(s32[64,1,4]{2,1,0:T(1,128)} %bitcast.1), calls=%async_computation | async-start | bytes 65536 | tf_op jit(solution)/shard_map/all_to_all | solution.py:144
  24.4 39.2 %copy-start.14 = (bf16[3584,256]{1,0:T(8,128)(2,1)}, bf16[3584,256]{1,0:T(8,128)(2,1)S(1)}, u32[]{:S(2)}) copy-start(bf16[3584,256]{1,0:T(8,128)(2,1)S(1)} %constant_dynamic-update-slice_fusion) | copy-start | bytes 5505028
  32.1 31.5 %copy-start.15 = (bf16[16,3584]{1,0:T(8,128)(2,1)S(1)}, bf16[16,3584]{1,0:T(8,128)(2,1)}, u32[]{:S(2)}) copy-start(bf16[16,3584]{1,0:T(8,128)(2,1)} %param.20) | copy-start | bytes 344068
  63.3 3.3 copy-start.18
  72.9 11.9 %copy-start.19 = (s32[4,8]{1,0:T(4,128)S(1)}, s32[4,8]{1,0:T(4,128)}, u32[]{:S(2)}) copy-start(s32[4,8]{1,0:T(4,128)} %param.23) | copy-start | bytes 388
  72.9 13.1 %copy-start.20 = (f32[512,8]{0,1:T(8,128)S(1)}, f32[512,8]{0,1:T(8,128)}, u32[]{:S(2)}) copy-start(f32[512,8]{0,1:T(8,128)} %param.25) | copy-start | bytes 49156
  72.9 13.1 %copy-start.21 = (bf16[896,8]{0,1:T(8,128)(2,1)S(1)}, bf16[896,8]{0,1:T(8,128)(2,1)}, u32[]{:S(2)}) copy-start(bf16[896,8]{0,1:T(8,128)(2,1)} %param.22) | copy-start | bytes 43012
  72.9 106.9 %all-to-all-start.1 = ((bf16[64,1,128,256]{3,2,1,0:T(8,128)(2,1)}), bf16[64,1,128,256]{3,2,1,0:T(8,128)(2,1)}, u32[]{:S(2)}, u32[]{:S(2)}) async-start(bf16[64,1,128,256]{3,2,1,0:T(8,128)(2,1)} %copy.96), calls=%async_computation.1 | async-start | bytes 8388608 | tf_op jit(solution)/shard_map/all_to_all | solution.py:150
  83.9 49.1 %all-gather.5.cloned.1.call-start = ((), (), s32[]{:S(2)}) async-start(), calls=%async_computation.4 | async-start | bytes 4587520 | tf_op jit(solution)/shard_map/all_gather | solution.py:94
  84.7 5.0 copy-start.22
  84.9 48.1 %copy-start.17 = (bf16[16,3584]{1,0:T(8,128)(2,1)S(1)}, bf16[16,3584]{1,0:T(8,128)(2,1)}, u32[]{:S(2)}) copy-start(bf16[16,3584]{1,0:T(8,128)(2,1)} %param.18) | copy-start | bytes 344068
  133.0 3.4 copy-start.3
  150.2 29.6 %copy-start.16 = (f32[512,256]{0,1:T(8,128)}, f32[512,256]{0,1:T(8,128)S(1)}, u32[]{:S(2)}) copy-start(f32[512,256]{0,1:T(8,128)S(1)} %convolution_bitcast_fusion.1) | copy-start | bytes 1572868
  182.7 2.5 copy-start.4
  182.7 2.5 copy-start.8
  185.2 7.0 %copy-start.9 = (bf16[4,1024,128]{2,1,0:T(8,128)(2,1)}, bf16[4,1024,128]{2,1,0:T(8,128)(2,1)S(1)}, u32[]{:S(2)}) copy-start(bf16[4,1024,128]{2,1,0:T(8,128)(2,1)S(1)} %get-tuple-element.15) | copy-start | bytes 3145732
  185.2 7.0 %copy-start.5 = (pred[4,128,1152]{1,2,0:T(8,128)(4,1)S(1)}, pred[4,128,1152]{1,2,0:T(8,128)(4,1)}, u32[]{:S(2)}) copy-start(pred[4,128,1152]{1,2,0:T(8,128)(4,1)} %concatenate.30) | copy-start | bytes 1769476
  192.2 8.8 %copy-start.13 = (bf16[4,128,7,128]{1,3,2,0:T(8,128)(2,1)S(1)}, bf16[4,128,7,128]{1,3,2,0:T(8,128)(2,1)}, u32[]{:S(2)}) copy-start(bf16[4,128,7,128]{1,3,2,0:T(8,128)(2,1)} %copy.112) | copy-start | bytes 2752516
  209.4 1.5 copy-start.7
  221.1 101.8 %all-to-all-start.2 = ((f32[64,1,128,128]{3,2,1,0:T(8,128)}), f32[64,1,128,128]{3,2,1,0:T(8,128)}, u32[]{:S(2)}, u32[]{:S(2)}) async-start(f32[64,1,128,128]{3,2,1,0:T(8,128)} %copy.118), calls=%async_computation.2 | async-start | bytes 8388608 | tf_op jit(solution)/shard_map/all_to_all | solution.py:185
  227.1 294.0 %all-reduce.6.cloned.1.call-start = ((), (), s32[]{:S(2)}) async-start(), calls=%async_computation.5 | async-start | bytes 360448 | tf_op jit(solution)/shard_map/psum | solution.py:219
  228.1 3.2 copy-start.6
  231.3 11.8 %copy-start.10 = (bf16[4,1024,128]{2,1,0:T(8,128)(2,1)S(1)}, bf16[4,1024,128]{2,1,0:T(8,128)(2,1)}, u32[]{:S(2)}) copy-start(bf16[4,1024,128]{2,1,0:T(8,128)(2,1)} %copy-done.9) | copy-start | bytes 3145732
  243.1 13.4 %slice-start = ((f32[4,1152,128]{1,2,0:T(8,128)}), f32[4,128,128]{1,2,0:T(8,128)S(1)}, s32[]{:S(2)}) async-start(f32[4,1152,128]{1,2,0:T(8,128)} %copy-done.7), calls=%async_computation.6 | async-start | bytes 524288 | tf_op jit(solution)/shard_map/slice | solution.py:176
  254.3 2.6 copy-start.12
  257.9 85.8 %copy-start.1 = (bf16[512,896]{1,0:T(8,128)(2,1)S(1)}, bf16[512,896]{1,0:T(8,128)(2,1)}, u32[]{:S(2)}) copy-start(bf16[512,896]{1,0:T(8,128)(2,1)} %param.13) | copy-start | bytes 2752516
  259.1 85.7 %copy-start.2 = (bf16[512,896]{1,0:T(8,128)(2,1)S(1)}, bf16[512,896]{1,0:T(8,128)(2,1)}, u32[]{:S(2)}) copy-start(bf16[512,896]{1,0:T(8,128)(2,1)} %param.14) | copy-start | bytes 2752516
Sparse Core Ops, SparseCore 0:
  9.9 50.2 all-gather.2
  86.6 46.3 all-gather.4
  345.8 175.2 all-reduce.5
where the time goes:
time: 543 us; the launch traced here: 534 us
  waiting for transfers between devices  348 us (64%)
  matrix products  76.7 us (14%)
  local copies, waits for them, and re-layouts  40 us (7%)
  starting transfers between devices  30.1 us (6%)
  between operations  14.5 us (3%)
  blocking collectives  13.2 us (2%)
  other arithmetic  11.1 us (2%)
    psum x1, waiting for transfers between devices, local(): lax.psum((query_down_grad, query_up_grad, value_down_grad, value_up_grad)...  175 us
    all_to_all x1, waiting for transfers between devices, local(): lax.all_to_all(grad_buffer.reshape(peer_count, CAP, BLK, kv_width), 'tm',...  63.8 us
    all_gather x1, waiting for transfers between devices, local(): token_piece = lax.all_gather(slab_tokens, 'heads', axis=1, tiled=True)  42.1 us
    all_to_all x1, waiting for transfers between devices, local(): lax.all_to_all(outgoing, 'tm', split_axis=0, concat_axis=0, tiled=True)  29.4 us
    all_gather x1, waiting for transfers between devices, local(): memory_piece = lax.all_gather(memory, 'heads', axis=1, tiled=True)  28.1 us
    psum x1, blocking collectives, local(): lax.psum(jnp.dot(attended, tag_weight, preferred_element_type=jnp.float32...  13.2 us
    all_to_all x1, starting transfers between devices, local(): lax.all_to_all(requested, 'tm', split_axis=0, concat_axis=0, tiled=True)  13 us
    dot_general x1, matrix products, attend(): jnp.einsum('cngrk,cknd->crngd', probs_low, value_heads, preferred_element...  11.8 us
  transfers between devices with their start and end apart: 6, of which 6 were waited for; matrix products, arithmetic and copies ran while one was open for 11% of the time, Pallas kernels for 0%

commit v1 on v0

v1 whole, which is shorter than its diff:
```python
import functools
import jax, jax.numpy as jnp
from jax import lax
from jax.sharding import PartitionSpec as P
from jax.experimental import pallas as pl
from jax.experimental.pallas import tpu as pltpu
BLK=128; HD=128; TOP=8; RANK=16; TAGS=8
HIGHEST=lax.Precision.HIGHEST
NT=(((1,),(1,)),((),()))
TN=(((0,),(0,)),((),()))
f32=jnp.float32; bf16=jnp.bfloat16
MB=4; OWNERS=64; ROWS=272; CH=384
def attend_kernel(ret,bnd, q_ref, kl_ref, vl_ref, low_ref, gt_ref, tw_ref, twt_ref, qup_ref, vup_ref, pool_ref,
                  cols_ref, qug_ref, vug_ref, mcot_ref,
                  land, kk, vv, lt, qs, gm, gs, st, pb, sg, at, qg, vg, sems):
    c=pl.program_id(0)
    heads=q_ref.shape[1]//HD
    wide=heads*BLK
    nkeys=(TOP+1)*BLK
    def fetch(i):
        return pltpu.make_async_copy(pool_ref.at[ret[lax.div(i,TOP),lax.rem(i,TOP)]], land.at[i], sems.at[i])
    @pl.when(c==0)
    def _():
        def go(i,_):
            fetch(i).start(); return 0
        lax.fori_loop(0,4*TOP,go,0)
        qug_ref[...]=jnp.zeros_like(qug_ref)
        vug_ref[...]=jnp.zeros_like(vug_ref)
        mcot_ref[...]=jnp.zeros_like(mcot_ref)
    rows=pl.ds(pl.multiple_of(c*BLK,BLK),BLK)
    grads=gt_ref[:,rows]
    for h in range(heads):
        cols=slice(h*HD,(h+1)*HD)
        g=jnp.dot(tw_ref[cols,:].astype(f32),grads,precision=HIGHEST,preferred_element_type=f32).astype(bf16)
        gm[:,cols]=g
        gs[cols,:]=g.T
        qs[cols,:]=q_ref[rows,cols]
    for s in range(TOP):
        i=c*TOP+s
        fetch(i).wait()
        kk[s*BLK:(s+1)*BLK,:]=land[i,0:128,:]
        vv[s*BLK:(s+1)*BLK,:]=land[i,128:256,:]
        lt[:,s*BLK:(s+1)*BLK]=land[i,256:272,:]
    own=slice(TOP*BLK,nkeys)
    kk[own,:]=kl_ref[rows,:]
    vv[own,:]=vl_ref[rows,:]
    lt[:,own]=low_ref[RANK:,rows]
    edge=bnd[c]
    def p1(j,m):
        r=pl.ds(pl.multiple_of(j*CH,CH),CH)
        s=lax.dot_general(kk[r,:],qs[...],NT,preferred_element_type=f32)
        st[r,:]=s
        return jnp.maximum(m,jnp.max(s[:CH-BLK],axis=0,keepdims=True)), s
    m=jnp.full((1,wide),-jnp.inf,f32)
    scale=HD**-0.5
    n_ch=nkeys//CH
    for j in range(n_ch):
        r=slice(j*CH,(j+1)*CH)
        s=lax.dot_general(kk[r,:],qs[...],NT,preferred_element_type=f32)*scale
        if j==n_ch-1:
            key=lax.broadcasted_iota(jnp.int32,(BLK,BLK),0)
            row=lax.broadcasted_iota(jnp.int32,(BLK,BLK),1)
            seen=(key<=row)&((key>=edge)|(row<edge))
            bias=jnp.where(seen,0.0,-jnp.inf).astype(f32)
            bias=jnp.concatenate([bias]*heads,axis=1)
            last=s[CH-BLK:]+bias
            s=jnp.concatenate([s[:CH-BLK],last],axis=0)
        st[r,:]=s
        m=jnp.maximum(m,jnp.max(s,axis=0,keepdims=True))
    tot=jnp.zeros((1,wide),f32)
    for j in range(n_ch):
        r=slice(j*CH,(j+1)*CH)
        e=jnp.exp(st[r,:]-m)
        st[r,:]=e
        tot=tot+jnp.sum(e,axis=0,keepdims=True)
    inv=1.0/tot
    acc=jnp.zeros((HD,wide),f32)
    for j in range(n_ch):
        r=slice(j*CH,(j+1)*CH)
        p=st[r,:]*inv
        st[r,:]=p
        pl_=p.astype(bf16)
        pb[r,:]=pl_
        acc=acc+lax.dot_general(vv[r,:],pl_,TN,preferred_element_type=f32)
    att=acc.astype(bf16)
    at[...]=att
    dot_row=jnp.sum(gm[...].astype(f32)*att.astype(f32),axis=0,keepdims=True)
    logits=jnp.zeros((TAGS,BLK),f32)
    for h in range(heads):
        cols=slice(h*HD,(h+1)*HD)
        logits=logits+jnp.dot(twt_ref[:,cols],at[:,cols],preferred_element_type=f32)
    cols_ref[c,0:TAGS,:]=logits
    acc=jnp.zeros((HD,wide),f32)
    for j in range(n_ch):
        r=slice(j*CH,(j+1)*CH)
        pg=jnp.dot(vv[r,:],gm[...],preferred_element_type=f32)
        sgr=(st[r,:]*(pg-dot_row)*scale).astype(bf16)
        acc=acc+lax.dot_general(kk[r,:],sgr,TN,preferred_element_type=f32)
        vg[r,:]=jnp.dot(pb[r,:],gs[...],preferred_element_type=f32)
    qg[...]=acc.astype(bf16)
    qcot=jnp.zeros((RANK,BLK),f32)
    for h in range(heads):
        cols=slice(h*HD,(h+1)*HD)
        qgh=qg[:,cols]
        qcot=qcot+jnp.dot(qup_ref[:,cols],qgh,preferred_element_type=f32)
        qug_ref[:,cols]+=lax.dot_general(low_ref[:RANK,rows],qgh,NT,preferred_element_type=f32)
    cols_ref[c,TAGS:TAGS+RANK,:]=qcot
    cot=lax.dot_general(vup_ref[...].astype(f32),vg[...],NT,precision=HIGHEST,preferred_element_type=f32)
    cols_ref[c,TAGS+RANK:,:]=cot[:,own]
    for s in range(TOP):
        mcot_ref[lax.div(ret[c,s],MB)]+=cot[:,s*BLK:(s+1)*BLK]
    vug_ref[...]+=jnp.dot(lt[...].astype(f32),vg[...],precision=HIGHEST,preferred_element_type=f32)

def attend(retrieval,boundary,q,kl,vl,low_t,grad_t,tw,tw_t,qup,vup,pool):
    n=q.shape[0]; wide=q.shape[1]; nk=(TOP+1)*BLK; spans=n//BLK
    vm=pl.BlockSpec(memory_space=pltpu.VMEM)
    shp=lambda *s: jax.ShapeDtypeStruct(s,f32)
    return pl.pallas_call(attend_kernel,
        grid_spec=pltpu.PrefetchScalarGridSpec(num_scalar_prefetch=2,grid=(spans,),
            in_specs=[vm]*9+[pl.BlockSpec(memory_space=pl.ANY)],
            out_specs=[vm]*4,
            scratch_shapes=[pltpu.VMEM((spans*TOP,ROWS,HD),bf16),pltpu.VMEM((nk,HD),bf16),pltpu.VMEM((nk,HD),bf16),pltpu.VMEM((RANK,nk),bf16),
              pltpu.VMEM((wide,HD),bf16),pltpu.VMEM((HD,wide),bf16),pltpu.VMEM((wide,HD),bf16),
              pltpu.VMEM((nk,wide),f32),pltpu.VMEM((nk,wide),bf16),pltpu.VMEM((8,128),bf16),
              pltpu.VMEM((HD,wide),bf16),pltpu.VMEM((HD,wide),bf16),pltpu.VMEM((nk,HD),f32),
              pltpu.SemaphoreType.DMA((spans*TOP,))]),
        out_shape=[shp(spans,TAGS+2*RANK,BLK),shp(RANK,wide),shp(RANK,HD),shp(OWNERS,RANK,BLK)],
        compiler_params=pltpu.CompilerParams(vmem_limit_bytes=50*2**20,dimension_semantics=("arbitrary",)),
    )(retrieval,boundary,q,kl,vl,low_t,grad_t,tw,tw_t,qup,vup,pool)

X=4; Y=4; Z=8; ZC=16; MESH=pl.DeviceIdType.MESH

def place():
    t=lax.axis_index("tm"); y=lax.axis_index("heads")
    return lax.div(t,ZC), y, lax.rem(t,ZC)

def reduce_kernel(w_ref, cols_ref, qug_ref, vug_ref, mcot_ref, slab_ref, mem_ref,
                  logit_out, grad_out,
                  xbuf, tbuf, ybuf, mbuf, zbuf, mall, cbuf, csum, lall, call, g1, r1, x1, o1, g2, r2, x2, o2,
                  xs, ys, zs, ms, cs, ls, ks, a1, b1, d1, a2, b2, d2):
    x,y,q=place()
    def xp(k): return (lax.rem(x+k,X)*ZC+q, y)
    def yp(k): return (x*ZC+q, lax.rem(y+k,Y))
    def zp(k): return (x*ZC+lax.rem(q+k,ZC), y)
    def each(n,do):
        def body(k,_):
            do(k); return 0
        lax.fori_loop(1,n,body,0)
    def rc(src,dst,sems,k,dev):
        return pltpu.make_async_remote_copy(src_ref=src,dst_ref=dst,send_sem=sems.at[0,k],recv_sem=sems.at[1,k],device_id=dev,device_id_type=MESH)
    bar=pltpu.get_barrier_semaphore()
    each(X,lambda k: pl.semaphore_signal(bar,inc=1,device_id=xp(k),device_id_type=MESH))
    each(Y,lambda k: pl.semaphore_signal(bar,inc=1,device_id=yp(k),device_id_type=MESH))
    each(ZC,lambda k: pl.semaphore_signal(bar,inc=1,device_id=zp(k),device_id_type=MESH))
    pl.semaphore_wait(bar,X+Y+ZC-3)
    mx=lambda k: rc(mcot_ref.at[pl.ds(lax.rem(x+k,X)*ZC,ZC)],xbuf.at[k],xs,k,xp(k))
    cy=lambda k: rc(cols_ref.at[lax.rem(y+k,Y)],cbuf.at[k],cs,k,yp(k))
    each(Y,lambda k: cy(k).start())
    each(X,lambda k: mx(k).start())
    each(Y,lambda k: cy(k).wait())
    total=cols_ref[y]+cbuf[1]+cbuf[2]+cbuf[3]
    lall[y]=total[:TAGS]
    call[y]=total[TAGS:].astype(bf16)
    ly=lambda k: rc(lall.at[y],lall.at[y],ls,k,yp(k))
    ky=lambda k: rc(call.at[y],call.at[y],ks,k,yp(k))
    each(Y,lambda k: ky(k).start())
    each(Y,lambda k: ly(k).start())
    each(X,lambda k: mx(k).wait())
    def expand(o,_):
        parts=[mcot_ref[x*ZC+o]]+[xbuf[k,o] for k in range(1,X)]
        for m in range(MB):
            acc=parts[0]*w_ref[x,o*MB+m]
            for k in range(1,X):
                acc=acc+parts[k]*w_ref[lax.rem(x+X-k,X),o*MB+m]
            tbuf[m,o]=acc
        return 0
    lax.fori_loop(0,ZC,expand,0)
    ty=lambda k: rc(tbuf.at[lax.rem(y+k,Y)],ybuf.at[k],ys,k,yp(k))
    each(Y,lambda k: ty(k).start())
    each(Y,lambda k: ky(k).wait())
    def split(ref,first,value):
        for j in range(value.shape[1]//128):
            ref[first+2*j]=value[0:8,j*128:(j+1)*128]
            ref[first+2*j+1]=value[8:16,j*128:(j+1)*128]
    qdg=jnp.zeros(qug_ref.shape,f32); vdg=jnp.zeros(qug_ref.shape,f32)
    for s in range(Y):
        piece=slab_ref[s*BLK:(s+1)*BLK,:]
        qdg=qdg+jnp.dot(call[s,0:RANK],piece,preferred_element_type=f32)
        vdg=vdg+jnp.dot(call[s,RANK:],piece,preferred_element_type=f32)
    split(g1,0,qdg); split(g1,14,qug_ref[...]); split(g1,28,vug_ref[...])
    g1[30]=jnp.zeros((8,128),f32); g1[31]=jnp.zeros((8,128),f32)
    ga=lambda k: rc(g1.at[pl.ds(lax.rem(q+k,ZC)*2,2)],r1.at[k],a1,k,zp(k))
    each(ZC,lambda k: ga(k).start())
    each(Y,lambda k: ty(k).wait())
    def ysum(o,_):
        mbuf[o]=tbuf[y,o]+ybuf[1,o]+ybuf[2,o]+ybuf[3,o]
        return 0
    lax.fori_loop(0,ZC,ysum,0)
    mz=lambda k: rc(mbuf.at[lax.rem(q+k,ZC)],zbuf.at[k],zs,k,zp(k))
    each(ZC,lambda k: mz(k).start())
    each(ZC,lambda k: ga(k).wait())
    acc=g1[pl.ds(q*2,2)]
    for k in range(1,ZC): acc=acc+r1[k]
    x1[x]=acc
    gb=lambda k: rc(x1.at[x],x1.at[x],b1,k,xp(k))
    each(X,lambda k: gb(k).start())
    each(ZC,lambda k: mz(k).wait())
    acc=mbuf[q]
    for k in range(1,ZC): acc=acc+zbuf[k]
    mall[y]=acc.astype(bf16)
    my=lambda k: rc(mall.at[y],mall.at[y],ms,k,yp(k))
    each(Y,lambda k: my(k).start())
    each(X,lambda k: gb(k).wait())
    o1[q]=x1[0]+x1[1]+x1[2]+x1[3]
    gd=lambda k: rc(o1.at[q],o1.at[q],d1,k,zp(k))
    each(ZC,lambda k: gd(k).start())
    each(Y,lambda k: my(k).wait())
    for m in range(MB):
        vdg=vdg+jnp.dot(mall[m],mem_ref[m*BLK:(m+1)*BLK,:],preferred_element_type=f32)
    split(g2,0,vdg)
    g2[14]=jnp.zeros((8,128),f32); g2[15]=jnp.zeros((8,128),f32)
    ha=lambda k: rc(g2.at[lax.rem(q+k,ZC)],r2.at[k],a2,k,zp(k))
    each(ZC,lambda k: ha(k).start())
    each(ZC,lambda k: ha(k).wait())
    acc=g2[q]
    for k in range(1,ZC): acc=acc+r2[k]
    x2[x]=acc
    hb=lambda k: rc(x2.at[x],x2.at[x],b2,k,xp(k))
    each(X,lambda k: hb(k).start())
    each(X,lambda k: hb(k).wait())
    o2[q]=x2[0]+x2[1]+x2[2]+x2[3]
    hd=lambda k: rc(o2.at[q],o2.at[q],d2,k,zp(k))
    each(ZC,lambda k: hd(k).start())
    each(Y,lambda k: ly(k).wait())
    for s in range(Y):
        logit_out[:,s*BLK:(s+1)*BLK]=lall[s]
    each(ZC,lambda k: gd(k).wait())
    for k in range(15):
        for i in range(2):
            grad_out[i*8:(i+1)*8,k*128:(k+1)*128]=o1[k,i]
    each(ZC,lambda k: hd(k).wait())
    for k in range(14):
        grad_out[(k%2)*8:(k%2)*8+8,(15+k//2)*128:(16+k//2)*128]=o2[k]

def reduce_all(w,cols,qug,vug,mcot,slab,mem):
    vm=pl.BlockSpec(memory_space=pltpu.VMEM)
    wide=qug.shape[1]
    V=pltpu.VMEM
    sem=lambda n: pltpu.SemaphoreType.DMA((2,n))
    return pl.pallas_call(reduce_kernel,
        in_specs=[pl.BlockSpec(memory_space=pltpu.SMEM)]+[vm]*6,
        out_specs=[vm,vm],
        out_shape=[jax.ShapeDtypeStruct((TAGS,slab.shape[0]),f32),jax.ShapeDtypeStruct((RANK,3*wide+HD),f32)],
        scratch_shapes=[V((X,ZC,RANK,BLK),f32),V((MB,ZC,RANK,BLK),f32),V((Y,ZC,RANK,BLK),f32),V((ZC,RANK,BLK),f32),V((ZC,RANK,BLK),f32),V((MB,RANK,BLK),bf16),
            V((Y,TAGS+2*RANK,BLK),f32),V((8,128),f32),V((Y,TAGS,BLK),f32),V((Y,2*RANK,BLK),bf16),
            V((32,8,128),f32),V((ZC,2,8,128),f32),V((X,2,8,128),f32),V((ZC,2,8,128),f32),
            V((16,8,128),f32),V((ZC,8,128),f32),V((X,8,128),f32),V((ZC,8,128),f32),
            sem(X),sem(Y),sem(ZC),sem(Y),sem(Y),sem(Y),sem(Y),sem(ZC),sem(X),sem(ZC),sem(ZC),sem(X),sem(ZC)],
        compiler_params=pltpu.CompilerParams(collective_id=1,has_side_effects=True,vmem_limit_bytes=32*2**20),
    )(w,cols,qug,vug,mcot,slab,mem)

def local(slab_tokens,memory,query_weight,key_weight,value_weight,query_down,query_up,value_down,value_up,tag_weight,retrieval,boundary,grad_tags):
    x,y,q=place()
    every=lax.all_gather(retrieval,"tm",axis=0,tiled=True).reshape(OWNERS,-1)
    mine=jnp.stack([lax.dynamic_index_in_dim(every,k*ZC+q,0,False) for k in range(X)])
    blocks=x*ZC*MB+jnp.arange(ZC*MB,dtype=jnp.int32)
    w=jnp.any(mine[:,:,None]==blocks[None,None,:],axis=1).astype(f32)
    pair_weight=jnp.concatenate([key_weight,value_weight],1)
    adapter_pair=jnp.concatenate([query_down,value_down],0)
    mem_full=lax.all_gather(memory,"heads",axis=1,tiled=True)
    tok_full=lax.all_gather(slab_tokens,"heads",axis=1,tiled=True)
    dot=lambda a,b: jnp.dot(a,b,preferred_element_type=f32)
    pair=lambda full,low: (dot(full,pair_weight)+jnp.pad(dot(low,value_up),((0,0),(HD,0)))).astype(bf16)
    mem_low=lax.dot_general(mem_full,value_down,NT,preferred_element_type=f32).astype(bf16)
    mem_pair=pair(mem_full,mem_low).reshape(MB,BLK,2*HD)
    piece=jnp.concatenate([mem_pair[:,:,:HD],mem_pair[:,:,HD:],mem_low.reshape(MB,BLK,RANK).transpose(0,2,1)],1)
    pool=lax.all_gather(piece,"tm",axis=0,tiled=True)
    low_t=lax.dot_general(adapter_pair,tok_full,NT,preferred_element_type=f32).astype(bf16)
    tok_pair=pair(tok_full,low_t[RANK:].T)
    queries=(dot(tok_full,query_weight)+dot(low_t[:RANK].T,query_up)).astype(bf16)
    cols,qug,vug,mcot=attend(retrieval,boundary,queries,tok_pair[:,:HD],tok_pair[:,HD:],low_t,grad_tags.T,tag_weight,tag_weight.T,query_up,value_up,pool)
    logits,grads=reduce_all(w,cols,qug,vug,mcot,slab_tokens,memory)
    wide=qug.shape[1]
    return logits.T,grads[:,:wide],grads[:,wide:2*wide],grads[:,2*wide+HD:],grads[:,2*wide:2*wide+HD]


def solution(mesh):
    in_specs=(P("tm","heads"),P("tm","heads"),P(None,"heads"),P(None,"heads"),P(None,"heads"),P(),P(None,"heads"),P(),P(None,"heads"),P("heads",None),P("tm",None),P("tm"),P("tm",None))
    out_specs=(P("tm",None),P(None,"heads"),P(None,"heads"),P(None,"heads"),P(None,"heads"))
    return jax.shard_map(local,mesh=mesh,in_specs=in_specs,out_specs=out_specs,check_vma=False)
```

time: 543 us -> 294 us (0.54); the launches traced: 534 us -> 294 us
  waiting for transfers between devices: 348 us -> 133 us
  Pallas kernels: 0 us -> 70.2 us
  matrix products: 76.7 us -> 19.7 us
  blocking collectives: 13.2 us -> 51.2 us
  local copies, waits for them, and re-layouts: 40 us -> 4.38 us
  starting transfers between devices: 30.1 us -> 0.11 us
  other arithmetic: 11.1 us -> 0.85 us
    psum x1 -> x0, waiting for transfers between devices: 175 us -> none  [local(): lax.psum((query_down_grad, query_up_grad, value_down_grad, value_up_grad)...]
    all_to_all x3 -> x0, waiting for transfers between devices: 101 us -> none  [the longest x1 63.8 us: local(): lax.all_to_all(grad_buffer.reshape(peer_count, CAP, BLK, kv_width), 'tm',...]
    pallas_call x0 -> x2, Pallas kernels: none -> 70.2 us  [the longest x1 46 us: reduce_all(): pl.pallas_call(reduce_kernel, in_specs=[pl.BlockSpec(memory_space=pltpu.S...]
    all_gather x2 -> x3, waiting for transfers between devices: 70.2 us -> 132 us  [the longest x1 81.7 us: local(): pool = lax.all_gather(piece, 'tm', axis=0, tiled=True)]
    dot_general x26 -> x8, matrix products: 76.7 us -> 19.7 us  [the longest x6 13.3 us: local(): dot = lambda a, b: jnp.dot(a, b, preferred_element_type=f32)]
    all_gather x0 -> x1, blocking collectives: none -> 51.2 us  [local(): lax.all_gather(retrieval, 'tm', axis=0, tiled=True).reshape(OWNERS, -1)]
    all_to_all x3 -> x0, starting transfers between devices: 29.9 us -> none  [the longest x1 13 us: local(): lax.all_to_all(requested, 'tm', split_axis=0, concat_axis=0, tiled=True)]
    psum x1 -> x0, blocking collectives: 13.2 us -> none  [local(): lax.psum(jnp.dot(attended, tag_weight, preferred_element_type=jnp.float32...]
  transfers between devices with their start and end apart: 6 -> 3, of which waited for: 6 -> 2; matrix products, arithmetic and copies ran while one was open for 11% -> 8% of each run, Pallas kernels for 0% -> 0%
where the time goes in v1:
time: 294 us
  waiting for transfers between devices  133 us (45%)
  Pallas kernels  70.2 us (24%)
  blocking collectives  51.2 us (17%)
  matrix products  19.7 us (7%)
  between operations  14.1 us (5%)
  local copies, waits for them, and re-layouts  4.38 us (1%)
    all_gather x1, waiting for transfers between devices, local(): pool = lax.all_gather(piece, 'tm', axis=0, tiled=True)  81.7 us
    all_gather x1, blocking collectives, local(): lax.all_gather(retrieval, 'tm', axis=0, tiled=True).reshape(OWNERS, -1)  51.2 us
    all_gather x1, waiting for transfers between devices, local(): mem_full = lax.all_gather(memory, 'heads', axis=1, tiled=True)  49.8 us
    pallas_call x1, Pallas kernels, reduce_all(): pl.pallas_call(reduce_kernel, in_specs=[pl.BlockSpec(memory_space=pltpu.S...  46 us
    pallas_call x1, Pallas kernels, attend(): pl.pallas_call(attend_kernel, grid_spec=pltpu.PrefetchScalarGridSpec(num_...  24.3 us
    dot_general x6, matrix products, local(): dot = lambda a, b: jnp.dot(a, b, preferred_element_type=f32)  13.3 us
  transfers between devices with their start and end apart: 3, of which 2 were waited for; matrix products, arithmetic and copies ran while one was open for 8% of the time, Pallas kernels for 0%

profile of v1, /device:TPU:1, one launch (start us, length us, event | category | flops | bytes accessed | tf_op | source)
XLA Modules:
  0.0 293.5 jit_solution(5527409345300484315)
XLA Ops:
  7.2 0.7 all-gather.7.cloned.1.call-update
  7.9 0.0 all-gather.5.cloned.1.call-start
  8.0 0.7 all-gather.5.cloned.1.call-update
  8.7 0.0 all-gather.9.cloned.1.call-start
  8.7 1.3 constant_dynamic-update-slice_fusion.1
  10.1 0.2 constant_dynamic-update-slice_fusion
  10.3 49.8 %all-gather.7.cloned.1.call-done = bf16[512,3584]{1,0:T(8,128)(2,1)} async-done(((bf16[512,896]{1,0:T(8,128)(2,1)}), bf16[512,3584]{1,0:T(8,128)(2,1)}) %all-gather.7.cloned.1.call-update) | async-done | bytes 3670032 | tf_op jit(solution)/shard_map/all_gather | solution.py:270
  60.1 3.1 %convolution_convert_fusion.1 = bf16[512,16]{0,1:T(8,128)(2,1)S(1)} fusion(bf16[512,3584]{1,0:T(8,128)(2,1)} %all-gather.7.cloned.1.call-done, bf16[16,3584]{1,0:T(8,128)(2,1)S(1)} %copy-done.10), kind=kOutput, calls=%fused_computation.8 | convolution fusion | flops 58728448 | bytes 3801088 | tf_op jit(solution)/shard_map/dot_general | solution.py:274
  63.3 0.2 fusion.15
  63.5 3.2 %fusion.3 = bf16[512,256]{0,1:T(8,128)(2,1)S(1)} fusion(bf16[3584,256]{1,0:T(8,128)(2,1)S(1)} %constant_dynamic-update-slice_fusion, bf16[512,3584]{1,0:T(8,128)(2,1)} %all-gather.7.cloned.1.call-done, f32[512,128]{0,1:T(8,128)S(1)} %fusion.15), kind=kOutput, calls=%fused_computation.6 | convolution fusion | flops 939786240 | bytes 6029312 | tf_op jit(solution)/shard_map/dot_general | solution.py:272
  66.8 0.1 copy.53
  67.0 0.7 pad_maximum_fusion
  67.7 51.2 %all-gather = s32[64,4,8]{2,1,0:T(4,128)S(1)} all-gather(s32[1,4,8]{2,1,0:T(4,128)S(1)} %bitcast.37), channel_id=1, replica_groups=mesh['tm'=64,'heads'=4] {'tm'}, dimensions={0}, use_global_device_ids=true | all-gather | bytes 8320 | tf_op jit(solution)/shard_map/all_gather | solution.py:264
  119.0 0.1 copy.40
  119.0 0.1 constant_dynamic-slice_fusion.3
  119.1 0.1 copy.41
  119.2 0.1 copy.44
  119.3 0.1 copy.43
  119.4 0.1 copy.42
  119.5 0.1 compare_reduce_fusion
  119.6 0.2 copy.50.tw_ref
  119.8 3.3 %convolution_convert_fusion.low_ref = bf16[32,512]{1,0:T(8,128)(2,1)S(1)} fusion(bf16[512,3584]{1,0:T(8,128)(2,1)} %all-gather.5.cloned.1.call-done, bf16[16,3584]{1,0:T(8,128)(2,1)S(1)} %copy-done.10, bf16[16,3584]{1,0:T(8,128)(2,1)S(1)} %copy-done.11), kind=kOutput, calls=%fused_computation.7 | convolution fusion | flops 117915648 | bytes 3932160 | tf_op jit(solution)/shard_map/dot_general | solution.py:278
  123.2 0.2 fusion.7
  123.4 1.1 fusion.2
  124.6 8.0 %fusion.14 = f32[512,896]{1,0:T(8,128)S(1)} fusion(bf16[512,3584]{1,0:T(8,128)(2,1)S(1)} %copy-done.8, bf16[3584,896]{1,0:T(8,128)(2,1)} %param.15), kind=kOutput, calls=%fused_computation.29 | convolution fusion | flops 3288334336 | bytes 11927552 | tf_op jit(solution)/shard_map/dot_general | solution.py:272
  132.7 0.4 add_convert_fusion.q_ref
  133.1 81.7 %all-gather.9.cloned.1.call-done.pool_ref = bf16[256,272,128]{2,1,0:T(8,128)(2,1)} async-done(((bf16[4,272,128]{2,1,0:T(8,128)(2,1)}), bf16[256,272,128]{2,1,0:T(8,128)(2,1)}) %all-gather.9.cloned.1.call-update) | async-done | bytes 17825808 | tf_op jit(solution)/shard_map/all_gather | solution.py:277
  214.9 24.3 %shard_map.164 = (f32[4,40,128]{2,1,0:T(8,128)S(1)}, f32[16,896]{1,0:T(8,128)S(1)}, f32[16,128]{1,0:T(8,128)S(1)}, f32[64,16,128]{2,1,0:T(8,128)S(1)}) custom-call(s32[4,8]{1,0:T(4,128)S(1)} %copy-done.6, s32[4]{0:T(128)S(1)} %copy-done.7, bf16[512,896]{1,0:T(8,128)(2,1)S(1)} %add_convert_fusion.q_ref, bf16[512,128]{1,0:T(8,128)(2,1)S(1)} %get-tuple-element.20.kl_ref, ...), custom_call_target="tpu_custom_call" | custom-call | tf_op jit(solution)/shard_map/pallas_call | solution.py:118
  239.1 46.0 %shard_map.165 = (f32[8,512]{1,0:T(8,128)S(1)}, f32[16,2816]{1,0:T(8,128)S(1)}) custom-call(f32[4,64]{1,0:T(4,128)S(1)} %convert_element_type.21.w_ref, f32[4,40,128]{2,1,0:T(8,128)S(1)} %get-tuple-element.11.cols_ref, f32[16,896]{1,0:T(8,128)S(1)} %get-tuple-element.12.qug_ref, f32[16,128]{1,0:T(8,128)S(1)} %get-tuple-element.13.vug_ref, ...), custom_call_target="tpu_custom_call" | custom-call | tf_op jit(solution)/shard_map/pallas_call | solution.py:250
  285.1 0.6 slice.39
  285.7 0.7 fusion.13
  286.4 0.6 copy.56
  (34 shorter events, 0.3 us)
Async XLA Ops:
  7.2 2.9 copy-start.9
  7.2 53.0 %copy-start.10 = (bf16[16,3584]{1,0:T(8,128)(2,1)S(1)}, bf16[16,3584]{1,0:T(8,128)(2,1)}, u32[]{:S(2)}) copy-start(bf16[16,3584]{1,0:T(8,128)(2,1)} %param.20) | copy-start | bytes 344068
  7.2 53.0 %all-gather.7.cloned.1.call-start = ((), (), s32[]{:S(2)}) async-start(), calls=%async_computation.1 | async-start | bytes 4587520 | tf_op jit(solution)/shard_map/all_gather | solution.py:270
  7.9 111.9 %all-gather.5.cloned.1.call-start = ((), (), s32[]{:S(2)}) async-start(), calls=%async_computation | async-start | bytes 4587520 | tf_op jit(solution)/shard_map/all_gather | solution.py:271
  8.7 206.2 %all-gather.9.cloned.1.call-start = ((), (), s32[]{:S(2)}) async-start(), calls=%async_computation.2 | async-start | bytes 18104320 | tf_op jit(solution)/shard_map/all_gather | solution.py:277
  10.1 53.2 %copy-start.4 = (bf16[16,128]{1,0:T(8,128)(2,1)S(1)}, bf16[16,128]{1,0:T(8,128)(2,1)}, u32[]{:S(2)}) copy-start(bf16[16,128]{1,0:T(8,128)(2,1)} %vup_ref.1) | copy-start | bytes 12292
  63.5 4.2 %copy-start.6 = (s32[4,8]{1,0:T(4,128)S(1)}, s32[4,8]{1,0:T(4,128)}, u32[]{:S(2)}) copy-start(s32[4,8]{1,0:T(4,128)} %ret.1) | copy-start | bytes 388
  63.5 56.1 %copy-start.3 = (bf16[896,8]{0,1:T(8,128)(2,1)S(1)}, bf16[896,8]{0,1:T(8,128)(2,1)}, u32[]{:S(2)}) copy-start(bf16[896,8]{0,1:T(8,128)(2,1)} %param.22) | copy-start | bytes 43012
  63.5 56.3 %copy-start.11 = (bf16[16,3584]{1,0:T(8,128)(2,1)S(1)}, bf16[16,3584]{1,0:T(8,128)(2,1)}, u32[]{:S(2)}) copy-start(bf16[16,3584]{1,0:T(8,128)(2,1)} %param.18) | copy-start | bytes 344068
  119.8 3.6 %copy-start.8 = (bf16[512,3584]{1,0:T(8,128)(2,1)S(1)}, bf16[512,3584]{1,0:T(8,128)(2,1)}, u32[]{:S(2)}) copy-start(bf16[512,3584]{1,0:T(8,128)(2,1)} %all-gather.5.cloned.1.call-done) | copy-start | bytes 11010052
  124.6 8.1 %copy-start.2 = (bf16[16,896]{1,0:T(8,128)(2,1)S(1)}, bf16[16,896]{1,0:T(8,128)(2,1)}, u32[]{:S(2)}) copy-start(bf16[16,896]{1,0:T(8,128)(2,1)} %qup_ref.1) | copy-start | bytes 86020
  124.6 90.3 %copy-start.5 = (f32[512,8]{0,1:T(8,128)S(1)}, f32[512,8]{0,1:T(8,128)}, u32[]{:S(2)}) copy-start(f32[512,8]{0,1:T(8,128)} %param.25) | copy-start | bytes 49156
  124.6 90.2 %copy-start.7 = (s32[4]{0:T(128)S(1)}, s32[4]{0:T(128)}, u32[]{:S(2)}) copy-start(s32[4]{0:T(128)} %bnd.1) | copy-start | bytes 52
  214.8 24.3 %copy-start = (bf16[512,896]{1,0:T(8,128)(2,1)S(1)}, bf16[512,896]{1,0:T(8,128)(2,1)}, u32[]{:S(2)}) copy-start(bf16[512,896]{1,0:T(8,128)(2,1)} %mem_ref.1) | copy-start | bytes 2752516
  214.8 24.3 %copy-start.1 = (bf16[512,896]{1,0:T(8,128)(2,1)S(1)}, bf16[512,896]{1,0:T(8,128)(2,1)}, u32[]{:S(2)}) copy-start(bf16[512,896]{1,0:T(8,128)(2,1)} %slab_ref.1) | copy-start | bytes 2752516
Sparse Core Ops, SparseCore 0:
  9.9 50.2 all-gather.6
  62.0 46.7 all-gather.4
  111.5 103.2 all-gather.8

commit v2 on v1

--- a/solution.py
+++ b/solution.py
@@ -169,9 +169,9 @@
     def expand(o,_):
         parts=[mcot_ref[x*ZC+o]]+[xbuf[k,o] for k in range(1,X)]
         for m in range(MB):
-            acc=parts[0]*w_ref[x,o*MB+m]
+            acc=parts[0]*w_ref[0,o*MB+m]
             for k in range(1,X):
-                acc=acc+parts[k]*w_ref[lax.rem(x+X-k,X),o*MB+m]
+                acc=acc+parts[k]*w_ref[k,o*MB+m]
             tbuf[m,o]=acc
         return 0
     lax.fori_loop(0,ZC,expand,0)
@@ -259,26 +259,200 @@
         compiler_params=pltpu.CompilerParams(collective_id=1,has_side_effects=True,vmem_limit_bytes=32*2**20),
     )(w,cols,qug,vug,mcot,slab,mem)
 
+UNITS=8
+
+def gather_kernel(mem_ref, slab_ref, wq_ref, wk_ref, wv_ref, qdown_ref, vdown_ref, qup_ref, vup_ref, ret_ref,
+                  pool, q_out, k_out, v_out, low_out, asked_out,
+                  feat, wq, wkv, stage, mine, ysem, ssem, rsem, lsem, osem, xsem):
+    t=lax.axis_index("tm"); y=lax.axis_index("heads")
+    x=lax.div(t,ZC); z=lax.rem(lax.div(t,2),Z); c=lax.rem(t,2)
+    def tm(xx,zz,cc): return (xx*Z+zz)*2+cc
+    def devx(k): return (tm(lax.rem(x+k,X),z,c),y)
+    def devz(d): return (tm(x,lax.rem(z+d+Z,Z),c),y)
+    devc=(tm(x,z,1-c),y)
+    def devy(d): return (t,lax.rem(y+d+Y,Y))
+    def loop(lo,hi,do):
+        def body(k,_):
+            do(k); return 0
+        lax.fori_loop(lo,hi,body,0)
+    bar=pltpu.get_barrier_semaphore()
+    def greet(dev): pl.semaphore_signal(bar,inc=1,device_id=dev,device_id_type=MESH)
+    loop(1,X,lambda k: greet(devx(k)))
+    for d in (1,-1):
+        greet(devz(d)); greet(devy(d))
+    greet(devc)
+    loads=[pltpu.make_async_copy(wk_ref,wkv.at[:,0:HD],lsem.at[0]),pltpu.make_async_copy(wv_ref,wkv.at[:,HD:2*HD],lsem.at[1]),pltpu.make_async_copy(wq_ref,wq,lsem.at[2])]
+    loads[0].start(); loads[1].start()
+    def rows_of(u):
+        return (mem_ref if u<MB else slab_ref).at[pl.ds((u%MB)*BLK,BLK)]
+    own=lambda u: pltpu.make_async_copy(rows_of(u),feat.at[u,y],osem.at[u])
+    for u in range(UNITS): own(u).start()
+    mine[...]=jnp.zeros_like(mine)
+    mine[0:MB,0:TOP]=ret_ref[...]
+    loads[2].start()
+    pl.semaphore_wait(bar,X-1+5)
+
+    def rc(src,dst,s,r,dev):
+        return pltpu.make_async_remote_copy(src_ref=src,dst_ref=dst,send_sem=s,recv_sem=r,device_id=dev,device_id_type=MESH)
+    left=lax.rem(y+Y-1,Y); right=lax.rem(y+1,Y); far=lax.rem(y+2,Y)
+    H=BLK//2
+    def y_first(u): return [rc(rows_of(u),feat.at[u,y],ysem.at[0,u,0],ysem.at[1,u,0],devy(1)),
+                            rc(rows_of(u),feat.at[u,y],ysem.at[0,u,1],ysem.at[1,u,1],devy(-1))]
+    def y_pass(u): return [rc(feat.at[u,left,pl.ds(0,H)],feat.at[u,left,pl.ds(0,H)],ysem.at[0,u,2],ysem.at[1,u,2],devy(1)),
+                           rc(feat.at[u,right,pl.ds(H,H)],feat.at[u,right,pl.ds(H,H)],ysem.at[0,u,3],ysem.at[1,u,3],devy(-1))]
+    def start(cs):
+        for cp in cs: cp.start()
+    asked=lambda k: rc(mine,asked_out.at[k],xsem.at[0,k],xsem.at[1,k],devx(k))
+
+    def bid(xx,zz,cc,b): return tm(xx,zz,cc)*MB+b
+    def at_x(k): return lax.rem(x+X-k,X)
+    def at_z(d,l): return lax.rem(z+Z-d*l,Z)
+    def sent(b,i): return ssem.at[b,i]
+    def share(b,i,g): rc(pool.at[g],pool.at[g],sent(b,i),rsem.at[g],devc).start()
+    def move(b,i,g,dev): rc(pool.at[g],pool.at[g],sent(b,i),rsem.at[g],dev).start()
+    def arrive(g): rc(pool.at[g],pool.at[g],ssem.at[0,0],rsem.at[g],devc).wait_recv()
+    def begin(b):
+        g=bid(x,z,c,b)
+        src=stage.at[b]
+        loop(1,X,lambda k: rc(src,pool.at[g],sent(b,k-1),rsem.at[g],devx(k)).start())
+        rc(src,pool.at[g],sent(b,3),rsem.at[g],devz(1)).start()
+        rc(src,pool.at[g],sent(b,4),rsem.at[g],devz(-1)).start()
+        rc(src,pool.at[g],sent(b,35),rsem.at[g],devc).start()
+        pltpu.make_async_copy(src,pool.at[g],lsem.at[3+b]).start()
+    def core0(b,phase):
+        if phase==1:
+            def go(k):
+                g=bid(at_x(k),z,0,b)
+                arrive(g)
+                move(b,3+2*k,g,devz(1)); move(b,4+2*k,g,devz(-1)); share(b,35+k,g)
+            loop(1,X,go)
+        elif phase in (2,3,4):
+            l=phase-1
+            def go(k):
+                xx=at_x(k)
+                for i,d in enumerate((1,-1)):
+                    g=bid(xx,at_z(d,l),0,b)
+                    arrive(g)
+                    if l<3:
+                        move(b,3+8*l+2*k+i,g,devz(d))
+                    else:
+                        pl.when((xx<2) if d==1 else (xx>=2))(lambda g=g,d=d: move(b,27+k,g,devz(d)))
+                    share(b,39+8*(l-1)+2*k+i,g)
+            loop(0,X,go)
+        else:
+            def go(k):
+                g=bid(at_x(k),at_z(1,4),0,b)
+                arrive(g)
+                share(b,63+k,g)
+            loop(0,X,go)
+    def core1(b,phase):
+        def spread(j,g):
+            loop(1,X,lambda k: move(b,8+3*j+k,g,devx(k)))
+        if phase in (1,2,3):
+            l=phase
+            for i,d in enumerate((1,-1)):
+                g=bid(x,at_z(d,l),1,b)
+                arrive(g)
+                if l<3: move(b,3+2*l+i,g,devz(d))
+                elif (b%2==0)==(d==1): move(b,9,g,devz(d))
+                spread(2*l-1+i,g)
+                share(b,35+2*l-1+i,g)
+        elif phase==4:
+            g=bid(x,at_z(1,4),1,b)
+            arrive(g); spread(7,g); share(b,35+7,g)
+        else:
+            def go(j):
+                k=lax.div(j,Z)+1
+                g=bid(at_x(k),lax.rem(z+j,Z),1,b)
+                arrive(g)
+                share(b,43+j,g)
+            loop(0,3*Z,go)
+    def step(b,phase):
+        pl.when(c==0)(lambda: core0(b,phase))
+        pl.when(c==1)(lambda: core1(b,phase))
+
+    def project(u):
+        own(u).wait()
+        if u==0:
+            loads[0].wait(); loads[1].wait()
+        if u==MB: loads[2].wait()
+        memory=u<MB
+        pair=jnp.zeros((BLK,2*HD),f32)
+        low=jnp.zeros((RANK if memory else 2*RANK,BLK),f32)
+        wide=wq.shape[1]
+        for h in range(Y):
+            cols=slice(h*wide,(h+1)*wide)
+            piece=feat[u,h]
+            pair=pair+jnp.dot(piece,wkv[cols,:],preferred_element_type=f32)
+            down=vdown_ref[:,cols] if memory else jnp.concatenate([qdown_ref[:,cols],vdown_ref[:,cols]],axis=0)
+            low=low+lax.dot_general(down,piece,NT,preferred_element_type=f32)
+        low=low.astype(bf16)
+        keys=pair[:,:HD].astype(bf16)
+        values=(pair[:,HD:]+lax.dot_general(low[-RANK:],vup_ref[...],TN,preferred_element_type=f32)).astype(bf16)
+        if memory:
+            stage[u,0:BLK,:]=keys
+            stage[u,BLK:2*BLK,:]=values
+            stage[u,2*BLK:,:]=low
+        else:
+            b=u-MB
+            rows=slice(b*BLK,(b+1)*BLK)
+            k_out[rows,:]=keys
+            v_out[rows,:]=values
+            low_out[:,rows]=low
+            acc=lax.dot_general(low[:RANK],qup_ref[...],TN,preferred_element_type=f32)
+            for h in range(Y):
+                acc=acc+jnp.dot(feat[u,h],wq[h*wide:(h+1)*wide,:],preferred_element_type=f32)
+            q_out[rows,:]=acc.astype(bf16)
+
+    start(y_first(0)); start(y_first(1))
+    loop(1,X,lambda k: asked(k).start())
+    asked_out[0]=mine[...]
+    middle={1:[(0,1),(0,2)],2:[(0,3),(0,4)],3:[(1,2)],4:[(1,4)],5:[(2,2)],6:[(2,4)],7:[(3,3)]}
+    end={2:[(0,5),(1,1)],3:[(1,3)],4:[(1,5),(2,1)],5:[(2,3)],6:[(2,5),(3,1),(3,2)],7:[(3,4),(3,5)]}
+    for u in range(UNITS):
+        for cp in y_first(u): cp.wait_recv()
+        start(y_pass(u))
+        if u+2<UNITS: start(y_first(u+2))
+        for b,p in middle.get(u,[]): step(b,p)
+        for cp in y_pass(u): cp.wait_recv()
+        project(u)
+        if u<MB: begin(u)
+        for b,p in end.get(u,[]): step(b,p)
+    loop(0,X*Z*MB,lambda j: arrive(bid(lax.div(j,Z*MB),lax.rem(lax.div(j,MB),Z),1-c,lax.rem(j,MB))))
+    loop(1,X,lambda k: asked(k).wait())
+    for u in range(UNITS):
+        for cp in y_first(u)+y_pass(u): cp.wait_send()
+    def gone(b,i): rc(stage.at[0],pool.at[0],ssem.at[b,i],rsem.at[0],devc).wait_send()
+    for b in range(MB):
+        pltpu.make_async_copy(stage.at[b],pool.at[0],lsem.at[3+b]).wait()
+        loop(35,67,lambda i: gone(b,i))
+        @pl.when(c==0)
+        def _():
+            loop(0,31,lambda i: gone(b,i))
+        @pl.when(c==1)
+        def _():
+            loop(0,10,lambda i: gone(b,i))
+            loop(12,33,lambda i: gone(b,i))
+
+def gather_all(mem,slab,wq,wk,wv,qdown,vdown,qup,vup,ret):
+    vm=pl.BlockSpec(memory_space=pltpu.VMEM); hbm=pl.BlockSpec(memory_space=pl.ANY)
+    n=slab.shape[0]; wide=wq.shape[1]
+    S=jax.ShapeDtypeStruct; V=pltpu.VMEM; D=pltpu.SemaphoreType.DMA
+    return pl.pallas_call(gather_kernel,
+        in_specs=[hbm]*5+[vm]*5,
+        out_specs=[hbm]+[vm]*5,
+        out_shape=[S((OWNERS*MB,ROWS,HD),bf16),S((n,wide),bf16),S((n,HD),bf16),S((n,HD),bf16),S((2*RANK,n),bf16),S((X,8,128),jnp.int32)],
+        scratch_shapes=[V((UNITS,Y,BLK,wide),bf16),V(wq.shape,bf16),V((wq.shape[0],2*HD),bf16),V((MB,ROWS,HD),bf16),V((8,128),jnp.int32),
+            D((2,UNITS,4)),D((MB,68)),D((OWNERS*MB,)),D((3+MB,)),D((UNITS,)),D((2,X))],
+        compiler_params=pltpu.CompilerParams(collective_id=2,has_side_effects=True,vmem_limit_bytes=40*2**20),
+    )(mem,slab,wq,wk,wv,qdown,vdown,qup,vup,ret)
+
 def local(slab_tokens,memory,query_weight,key_weight,value_weight,query_down,query_up,value_down,value_up,tag_weight,retrieval,boundary,grad_tags):
     x,y,q=place()
-    every=lax.all_gather(retrieval,"tm",axis=0,tiled=True).reshape(OWNERS,-1)
-    mine=jnp.stack([lax.dynamic_index_in_dim(every,k*ZC+q,0,False) for k in range(X)])
+    pool,queries,keys,values,low_t,asked=gather_all(memory,slab_tokens,query_weight,key_weight,value_weight,query_down,value_down,query_up,value_up,retrieval)
     blocks=x*ZC*MB+jnp.arange(ZC*MB,dtype=jnp.int32)
-    w=jnp.any(mine[:,:,None]==blocks[None,None,:],axis=1).astype(f32)
-    pair_weight=jnp.concatenate([key_weight,value_weight],1)
-    adapter_pair=jnp.concatenate([query_down,value_down],0)
-    mem_full=lax.all_gather(memory,"heads",axis=1,tiled=True)
-    tok_full=lax.all_gather(slab_tokens,"heads",axis=1,tiled=True)
-    dot=lambda a,b: jnp.dot(a,b,preferred_element_type=f32)
-    pair=lambda full,low: (dot(full,pair_weight)+jnp.pad(dot(low,value_up),((0,0),(HD,0)))).astype(bf16)
-    mem_low=lax.dot_general(mem_full,value_down,NT,preferred_element_type=f32).astype(bf16)
-    mem_pair=pair(mem_full,mem_low).reshape(MB,BLK,2*HD)
-    piece=jnp.concatenate([mem_pair[:,:,:HD],mem_pair[:,:,HD:],mem_low.reshape(MB,BLK,RANK).transpose(0,2,1)],1)
-    pool=lax.all_gather(piece,"tm",axis=0,tiled=True)
-    low_t=lax.dot_general(adapter_pair,tok_full,NT,preferred_element_type=f32).astype(bf16)
-    tok_pair=pair(tok_full,low_t[RANK:].T)
-    queries=(dot(tok_full,query_weight)+dot(low_t[:RANK].T,query_up)).astype(bf16)
-    cols,qug,vug,mcot=attend(retrieval,boundary,queries,tok_pair[:,:HD],tok_pair[:,HD:],low_t,grad_tags.T,tag_weight,tag_weight.T,query_up,value_up,pool)
+    w=jnp.any(asked[:,:MB,:TOP].reshape(X,-1)[:,:,None]==blocks[None,None,:],axis=1).astype(f32)
+    cols,qug,vug,mcot=attend(retrieval,boundary,queries,keys,values,low_t,grad_tags.T,tag_weight,tag_weight.T,query_up,value_up,pool)
     logits,grads=reduce_all(w,cols,qug,vug,mcot,slab_tokens,memory)
     wide=qug.shape[1]
     return logits.T,grads[:,:wide],grads[:,wide:2*wide],grads[:,2*wide+HD:],grads[:,2*wide:2*wide+HD]

time: 294 us -> 206 us (0.70)
  waiting for transfers between devices: 133 us -> 0 us
  Pallas kernels: 70.2 us -> 186 us
  blocking collectives: 51.2 us -> 0 us
  matrix products: 19.7 us -> 0 us
  local copies, waits for them, and re-layouts: 4.38 us -> 18.5 us
  between operations: 14.1 us -> 0.74 us
    all_gather x3 -> x0, waiting for transfers between devices: 132 us -> none  [the longest x1 81.7 us: local(): pool = lax.all_gather(piece, 'tm', axis=0, tiled=True)]
    pallas_call x0 -> x1, Pallas kernels: none -> 115 us  [gather_all(): pl.pallas_call(gather_kernel, in_specs=[hbm] * 5 + [vm] * 5, out_specs=[h...]
    all_gather x1 -> x0, blocking collectives: 51.2 us -> none  [local(): lax.all_gather(retrieval, 'tm', axis=0, tiled=True).reshape(OWNERS, -1)]
    dot_general x8 -> x0, matrix products: 19.7 us -> none  [the longest x6 13.3 us: local(): dot = lambda a, b: jnp.dot(a, b, preferred_element_type=f32)]
    unnamed x27 -> x38, local copies, waits for them, and re-layouts: 2.18 us -> 17.1 us
  transfers between devices with their start and end apart: 3 -> 0, of which waited for: 2 -> 0; matrix products, arithmetic and copies ran while one was open for 8% -> 0% of each run, Pallas kernels for 0% -> 0%
where the time goes in v2:
time: 206 us; the launch traced here: 205 us
  Pallas kernels  186 us (90%)
  local copies, waits for them, and re-layouts  18.5 us (9%)
    pallas_call x1, Pallas kernels, gather_all(): pl.pallas_call(gather_kernel, in_specs=[hbm] * 5 + [vm] * 5, out_specs=[h...  115 us
    pallas_call x1, Pallas kernels, reduce_all(): pl.pallas_call(reduce_kernel, in_specs=[pl.BlockSpec(memory_space=pltpu.S...  46.6 us
    pallas_call x1, Pallas kernels, attend(): pl.pallas_call(attend_kernel, grid_spec=pltpu.PrefetchScalarGridSpec(num_...  24.2 us
    unnamed x38, local copies, waits for them, and re-layouts  17.1 us

profile of v2, /device:TPU:1, one launch (start us, length us, event | category | flops | bytes accessed | tf_op | source)
XLA Modules:
  0.0 205.2 jit_solution(14175212155770235926)
XLA Ops:
  0.6 0.9 copy.19.tw_ref
  1.5 0.0 copy-start
  1.6 2.8 %copy-done = bf16[3584,896]{1,0:T(8,128)(2,1)S(1)} copy-done((bf16[3584,896]{1,0:T(8,128)(2,1)S(1)}, bf16[3584,896]{1,0:T(8,128)(2,1)}, u32[]{:S(2)}) %copy-start) | copy-done | bytes 6422552
  4.4 0.0 copy-start.1
  4.4 1.2 copy-done.1
  5.6 0.0 copy-start.3
  5.6 1.2 copy-done.3
  6.7 0.0 copy-start.5
  6.7 1.2 copy-done.5
  7.9 1.2 copy-done.6
  9.1 0.9 copy-done.7
  10.0 0.9 copy-done.8
  10.9 0.7 copy-done.9
  11.6 0.7 copy-done.13
  12.3 0.7 copy-done.15
  13.0 115.0 %shard_map.164 = (bf16[256,272,128]{2,1,0:T(8,128)(2,1)}, bf16[512,896]{1,0:T(8,128)(2,1)S(1)}, bf16[512,128]{1,0:T(8,128)(2,1)S(1)}, bf16[512,128]{1,0:T(8,128)...) custom-call(bf16[512,896]{1,0:T(8,128)(2,1)S(1)} %copy-done.1, bf16[512,896]{1,0:T(8,128)(2,1)S(1)} %copy-done.3, ...), custom_call_target="tpu_custom_call" | custom-call | tf_op jit(solution)/shard_map/pallas_call | solution.py:441
  128.0 0.1 eq.15
  128.1 0.1 compare_reduce_fusion
  128.2 0.0 copy-start.10
  128.2 0.7 copy-done.10
  129.0 0.7 copy-done.11
  129.7 0.7 copy-done.12
  130.4 0.7 copy-done.14
  131.1 0.7 copy-done.16
  131.8 0.7 copy-done.17
  132.4 24.2 %shard_map.165 = (f32[4,40,128]{2,1,0:T(8,128)S(1)}, f32[16,896]{1,0:T(8,128)S(1)}, f32[16,128]{1,0:T(8,128)S(1)}, f32[64,16,128]{2,1,0:T(8,128)S(1)}) custom-call(s32[4,8]{1,0:T(4,128)S(1)} %copy-done.16, s32[4]{0:T(128)S(1)} %copy-done.17, bf16[512,896]{1,0:T(8,128)(2,1)S(1)} %get-tuple-element.18.q_ref, bf16[512,128]{1,0:T(8,128)(2,1)S(1)} %get-tuple-element.19.kl_ref, ...), custom_call_target="tpu_custom_call" | custom-call | tf_op jit(solution)/shard_map/pallas_call | solution.py:118
  156.7 0.0 copy-done.2
  156.7 0.0 copy-done.4
  156.7 46.6 %shard_map.166 = (f32[8,512]{1,0:T(8,128)S(1)}, f32[16,2816]{1,0:T(8,128)S(1)}) custom-call(f32[4,64]{1,0:T(4,128)S(1)} %convert_element_type.3.w_ref, f32[4,40,128]{2,1,0:T(8,128)S(1)} %get-tuple-element.23.cols_ref, f32[16,896]{1,0:T(8,128)S(1)} %get-tuple-element.24.qug_ref, f32[16,128]{1,0:T(8,128)S(1)} %get-tuple-element.25.vug_ref, ...), custom_call_target="tpu_custom_call" | custom-call | tf_op jit(solution)/shard_map/pallas_call | solution.py:250
  203.3 0.6 slice.19
  203.9 0.7 fusion
  204.6 0.6 copy.21
  (16 shorter events, 0.0 us)
Async XLA Ops:
  1.5 2.8 %copy-start = (bf16[3584,896]{1,0:T(8,128)(2,1)S(1)}, bf16[3584,896]{1,0:T(8,128)(2,1)}, u32[]{:S(2)}) copy-start(bf16[3584,896]{1,0:T(8,128)(2,1)} %wq_ref.1) | copy-start | bytes 19267588
  4.4 1.2 copy-start.1
  5.6 1.2 copy-start.3
  6.7 1.2 copy-start.5
  7.9 1.2 copy-start.6
  9.1 0.9 copy-start.7
  10.0 0.9 copy-start.8
  10.9 0.7 copy-start.9
  11.6 0.7 copy-start.13
  12.3 0.7 copy-start.15
  13.0 143.7 %copy-start.2 = (bf16[512,896]{1,0:T(8,128)(2,1)S(1)}, bf16[512,896]{1,0:T(8,128)(2,1)}, u32[]{:S(2)}) copy-start(bf16[512,896]{1,0:T(8,128)(2,1)} %mem_ref.3) | copy-start | bytes 2752516
  13.0 143.7 %copy-start.4 = (bf16[512,896]{1,0:T(8,128)(2,1)S(1)}, bf16[512,896]{1,0:T(8,128)(2,1)}, u32[]{:S(2)}) copy-start(bf16[512,896]{1,0:T(8,128)(2,1)} %slab_ref.3) | copy-start | bytes 2752516
  128.2 0.8 copy-start.10
  129.0 0.7 copy-start.11
  129.7 0.7 copy-start.12
  130.4 0.7 copy-start.14
  131.1 0.7 copy-start.16
  131.8 0.7 copy-start.17

commit v3 on v1

v3 whole, which is shorter than its diff:
```python
import functools
import jax, jax.numpy as jnp
from jax import lax
from jax.sharding import PartitionSpec as P
from jax.experimental import pallas as pl
from jax.experimental.pallas import tpu as pltpu
BLK=128; HD=128; TOP=8; RANK=16; TAGS=8
HIGHEST=lax.Precision.HIGHEST
NT=(((1,),(1,)),((),()))
TN=(((0,),(0,)),((),()))
f32=jnp.float32; bf16=jnp.bfloat16
MB=4; OWNERS=64; ROWS=272; CH=384; X=4; Y=4; Z=8; ZC=16; LOG2E=1.4426950408889634; MESH=pl.DeviceIdType.MESH
def attend_kernel(ret,bnd, q_hbm, kl_hbm, vl_hbm, low_hbm, gt_hbm, twt_hbm, qup_hbm, vup_hbm, pool_ref,
                  cols_ref, qug_ref, vug_ref, mcot_ref,
                  q_ref, kl_ref, vl_ref, low_ref, gt_ref, twt_ref, qup_ref, vup_ref,
                  land, kk, vv, lt, qs, gm, gs, st, pb, at, qg, vg, mc, sems, lsem):
    c=pl.program_id(0)
    heads=q_ref.shape[1]//HD
    wide=heads*BLK
    nkeys=(TOP+1)*BLK
    z=lax.rem(lax.div(lax.axis_index("tm"),2),Z)
    def fetch(i):
        g=ret[lax.div(i,TOP),lax.rem(i,TOP)]
        o=lax.div(g,MB)
        d=lax.rem(lax.rem(lax.div(o,2),Z)+Z-z,Z)
        slot=jnp.where(d==0,0,jnp.where(d<Z//2,2*d,jnp.where(d==Z//2,Z-1,2*(Z-d)-1)))
        return pltpu.make_async_copy(pool_ref.at[lax.rem(g,MB),lax.rem(o,2),lax.div(o,ZC),slot], land.at[i], sems.at[i])
    loads=[pltpu.make_async_copy(src,dst,lsem.at[i]) for i,(src,dst) in enumerate([(q_hbm,q_ref),(kl_hbm,kl_ref),(vl_hbm,vl_ref),(low_hbm,low_ref),(gt_hbm,gt_ref),(twt_hbm,twt_ref),(qup_hbm,qup_ref),(vup_hbm,vup_ref)])]
    @pl.when(c==0)
    def _():
        for cp in loads: cp.start()
        def go(i,_):
            fetch(i).start(); return 0
        lax.fori_loop(0,4*TOP,go,0)
        qug_ref[...]=jnp.zeros_like(qug_ref)
        vug_ref[...]=jnp.zeros_like(vug_ref)
        mc[...]=jnp.zeros_like(mc)
        for cp in loads: cp.wait()
    rows=pl.ds(pl.multiple_of(c*BLK,BLK),BLK)
    part=gt_ref[:,rows]
    terms=[]
    for _ in range(3):
        low=part.astype(bf16).astype(f32)
        terms.append(low); part=part-low
    grads=jnp.concatenate(terms+[jnp.zeros_like(part)],axis=0).astype(bf16)
    tags=jnp.concatenate([twt_ref[...].astype(f32)]*4,axis=0).astype(bf16)
    across=lax.dot_general(tags,grads,TN,preferred_element_type=f32).astype(bf16)
    down=lax.dot_general(grads,tags,TN,preferred_element_type=f32).astype(bf16)
    for h in range(heads):
        cols=slice(h*HD,(h+1)*HD)
        gm[:,cols]=across[cols,:]
        gs[cols,:]=down[:,cols]
        qs[cols,:]=q_ref[rows,cols]
    for s in range(TOP):
        i=c*TOP+s
        fetch(i).wait()
        kk[s*BLK:(s+1)*BLK,:]=land[i,0:128,:]
        vv[s*BLK:(s+1)*BLK,:]=land[i,128:256,:]
        lt[:,s*BLK:(s+1)*BLK]=land[i,256:272,:]
    own=slice(TOP*BLK,nkeys)
    kk[own,:]=kl_ref[rows,:]
    vv[own,:]=vl_ref[rows,:]
    lt[:,own]=low_ref[RANK:,rows]
    edge=bnd[c]
    m=jnp.full((1,wide),-jnp.inf,f32)
    scale=HD**-0.5
    n_ch=nkeys//CH
    for j in range(n_ch):
        r=slice(j*CH,(j+1)*CH)
        s=lax.dot_general(kk[r,:],qs[...],NT,preferred_element_type=f32)
        if j==n_ch-1:
            key=lax.broadcasted_iota(jnp.int32,(BLK,BLK),0)
            row=lax.broadcasted_iota(jnp.int32,(BLK,BLK),1)
            seen=(key<=row)&((key>=edge)|(row<edge))
            bias=jnp.where(seen,0.0,-jnp.inf).astype(f32)
            bias=jnp.concatenate([bias]*heads,axis=1)
            last=s[CH-BLK:]+bias
            s=jnp.concatenate([s[:CH-BLK],last],axis=0)
        st[r,:]=s
        m=jnp.maximum(m,jnp.max(s,axis=0,keepdims=True))
    tot=jnp.zeros((1,wide),f32)
    for j in range(n_ch):
        r=slice(j*CH,(j+1)*CH)
        e=jnp.exp2((st[r,:]-m)*(scale*LOG2E))
        st[r,:]=e
        tot=tot+jnp.sum(e,axis=0,keepdims=True)
    inv=1.0/tot
    acc=jnp.zeros((HD,wide),f32)
    for j in range(n_ch):
        r=slice(j*CH,(j+1)*CH)
        pl_=(st[r,:]*inv).astype(bf16)
        pb[r,:]=pl_
        acc=acc+lax.dot_general(vv[r,:],pl_,TN,preferred_element_type=f32)
    att=acc.astype(bf16)
    at[...]=att
    dot_row=jnp.sum(gm[...].astype(f32)*att.astype(f32),axis=0,keepdims=True)
    inv=inv*scale
    acc=jnp.zeros((HD,wide),f32)
    for j in range(n_ch):
        r=slice(j*CH,(j+1)*CH)
        pg=jnp.dot(vv[r,:],gm[...],preferred_element_type=f32)
        sgr=((st[r,:]*inv)*(pg-dot_row)).astype(bf16)
        acc=acc+lax.dot_general(kk[r,:],sgr,TN,preferred_element_type=f32)
        vg[r,:]=jnp.dot(pb[r,:],gs[...],preferred_element_type=f32)
    qg[...]=acc.astype(bf16)
    logits=jnp.zeros((TAGS,BLK),f32)
    qcot=jnp.zeros((RANK,BLK),f32)
    for h in range(heads):
        cols=slice(h*HD,(h+1)*HD)
        qgh=qg[:,cols]
        logits=logits+jnp.dot(twt_ref[:,cols],at[:,cols],preferred_element_type=f32)
        qcot=qcot+jnp.dot(qup_ref[:,cols],qgh,preferred_element_type=f32)
        qug_ref[:,cols]+=lax.dot_general(low_ref[:RANK,rows],qgh,NT,preferred_element_type=f32)
    cols_ref[c,0:TAGS,:]=logits
    cols_ref[c,TAGS:TAGS+RANK,:]=qcot
    whole=vg[...]
    high=whole.astype(bf16)
    rest=(whole-high.astype(f32)).astype(bf16)
    up=vup_ref[...]
    cot=lax.dot_general(up,high,NT,preferred_element_type=f32)+lax.dot_general(up,rest,NT,preferred_element_type=f32)
    cols_ref[c,TAGS+RANK:,:]=cot[:,own]
    for s in range(TOP):
        o=lax.div(ret[c,s],MB)
        zo=lax.rem(lax.div(o,2),Z)
        mc[lax.div(o,ZC)*ZC+lax.rem(zo,Y)*4+lax.div(zo,Y)*2+lax.rem(o,2)]+=cot[:,s*BLK:(s+1)*BLK]
    side=lt[...]
    vug_ref[...]+=jnp.dot(side,high,preferred_element_type=f32)+jnp.dot(side,rest,preferred_element_type=f32)
    @pl.when(c==pl.num_programs(0)-1)
    def _():
        mcot_ref[...]=mc[...].astype(bf16)

def attend(retrieval,boundary,q,kl,vl,low_t,grad_t,tw_t,qup,vup,pool):
    n=q.shape[0]; wide=q.shape[1]; nk=(TOP+1)*BLK; spans=n//BLK
    vm=pl.BlockSpec(memory_space=pltpu.VMEM)
    V=pltpu.VMEM
    shp=lambda *s: jax.ShapeDtypeStruct(s,f32)
    return pl.pallas_call(attend_kernel,
        grid_spec=pltpu.PrefetchScalarGridSpec(num_scalar_prefetch=2,grid=(spans,),
            in_specs=[pl.BlockSpec(memory_space=pl.ANY)]*9,
            out_specs=[vm]*4,
            scratch_shapes=[V(a.shape,a.dtype) for a in (q,kl,vl,low_t,grad_t,tw_t,qup,vup)]+[
              V((spans*TOP,ROWS,HD),bf16),V((nk,HD),bf16),V((nk,HD),bf16),V((RANK,nk),bf16),
              V((wide,HD),bf16),V((HD,wide),bf16),V((wide,HD),bf16),
              V((nk,wide),f32),V((nk,wide),bf16),
              V((HD,wide),bf16),V((HD,wide),bf16),V((nk,HD),f32),V((OWNERS,RANK,BLK),f32),
              pltpu.SemaphoreType.DMA((spans*TOP,)),pltpu.SemaphoreType.DMA((8,))]),
        out_shape=[shp(spans,TAGS+2*RANK,BLK),shp(RANK,wide),shp(RANK,HD),jax.ShapeDtypeStruct((OWNERS,RANK,BLK),bf16)],
        compiler_params=pltpu.CompilerParams(vmem_limit_bytes=60*2**20,dimension_semantics=("arbitrary",)),
    )(retrieval,boundary,q,kl,vl,low_t,grad_t,tw_t,qup,vup,pool)

def place():
    t=lax.axis_index("tm"); y=lax.axis_index("heads")
    return lax.div(t,ZC), y, lax.rem(t,ZC)

def reduce_kernel(w_ref, cols_ref, qug_ref, vug_ref, mcot_ref, slab_hbm, mem_hbm,
                  logit_out, grad_out,
                  slab_ref, mem_ref, xbuf, tbuf, zbuf, mall, cbuf, lall, call, g1, r1, x1, o1, g2, r2, x2, o2,
                  xs, ys, zs, ms, cs, ls, ks, a1, b1, d1, a2, b2, d2, lsem):
    x,y,q=place()
    def xp(k): return (lax.rem(x+k,X)*ZC+q, y)
    def yp(k): return (x*ZC+q, lax.rem(y+k,Y))
    def zp(k): return (x*ZC+lax.rem(q+k,ZC), y)
    def xyp(k): return (lax.rem(x+lax.div(k,Y),X)*ZC+q, lax.rem(y+lax.rem(k,Y),Y))
    def each(n,do):
        def body(k,_):
            do(k); return 0
        lax.fori_loop(1,n,body,0)
    def rc(src,dst,sems,k,dev):
        return pltpu.make_async_remote_copy(src_ref=src,dst_ref=dst,send_sem=sems.at[0,k],recv_sem=sems.at[1,k],device_id=dev,device_id_type=MESH)
    loads=[pltpu.make_async_copy(slab_hbm,slab_ref,lsem.at[0]),pltpu.make_async_copy(mem_hbm,mem_ref,lsem.at[1])]
    for cp in loads: cp.start()
    bar=pltpu.get_barrier_semaphore()
    each(X*Y,lambda k: pl.semaphore_signal(bar,inc=1,device_id=xyp(k),device_id_type=MESH))
    each(ZC,lambda k: pl.semaphore_signal(bar,inc=1,device_id=zp(k),device_id_type=MESH))
    pl.semaphore_wait(bar,X*Y+ZC-2)
    def slots(k): return pl.ds(lax.rem(x+lax.div(k,Y),X)*ZC+lax.rem(y+lax.rem(k,Y),Y)*4,4)
    mx=lambda k: rc(mcot_ref.at[slots(k)],xbuf.at[k],xs,k,xyp(k))
    cy=lambda k: rc(cols_ref.at[lax.rem(y+k,Y)],cbuf.at[k],cs,k,yp(k))
    each(X*Y,lambda k: mx(k).start())
    each(Y,lambda k: cy(k).start())
    each(Y,lambda k: cy(k).wait())
    total=cols_ref[y]+cbuf[1]+cbuf[2]+cbuf[3]
    lall[y]=total[:TAGS]
    call[y]=total[TAGS:].astype(bf16)
    ly=lambda k: rc(lall.at[y],lall.at[y],ls,k,yp(k))
    ky=lambda k: rc(call.at[y],call.at[y],ks,k,yp(k))
    each(Y,lambda k: ky(k).start())
    each(Y,lambda k: ly(k).start())
    xbuf[0]=mcot_ref[slots(0)]
    each(X*Y,lambda k: mx(k).wait())
    def owner(j):
        half,core=(j//2,j%2) if isinstance(j,int) else (lax.div(j,2),lax.rem(j,2))
        return (y+Y*half)*2+core
    def expand(j,_):
        parts=[]
        for k in range(X):
            s=xbuf[Y*k,j].astype(f32)
            for i in range(1,Y): s=s+xbuf[Y*k+i,j].astype(f32)
            parts.append(s)
        for m in range(MB):
            at=owner(j)*MB+m
            acc=parts[0]*w_ref[0,at]
            for k in range(1,X):
                acc=acc+parts[k]*w_ref[k,at]
            tbuf[j,m]=acc.astype(bf16)
        return 0
    lax.fori_loop(0,4,expand,0)
    home=lax.rem(lax.div(q,2),Y)==y
    for j in range(4):
        @pl.when(owner(j)!=q)
        def _():
            pltpu.make_async_remote_copy(src_ref=tbuf.at[j],dst_ref=zbuf.at[q],send_sem=ys.at[0,j],recv_sem=zs.at[1,q],device_id=(x*ZC+owner(j),y),device_id_type=MESH).start()
    each(Y,lambda k: ky(k).wait())
    def split(ref,first,value):
        for j in range(value.shape[1]//128):
            ref[first+2*j]=value[0:8,j*128:(j+1)*128]
            ref[first+2*j+1]=value[8:16,j*128:(j+1)*128]
    qdg=jnp.zeros(qug_ref.shape,f32); vdg=jnp.zeros(qug_ref.shape,f32)
    loads[0].wait()
    for s in range(Y):
        piece=slab_ref[s*BLK:(s+1)*BLK,:]
        qdg=qdg+jnp.dot(call[s,0:RANK],piece,preferred_element_type=f32)
        vdg=vdg+jnp.dot(call[s,RANK:],piece,preferred_element_type=f32)
    split(g1,0,qdg); split(g1,14,qug_ref[...]); split(g1,28,vug_ref[...])
    g1[30]=jnp.zeros((8,128),f32); g1[31]=jnp.zeros((8,128),f32)
    ga=lambda k: rc(g1.at[pl.ds(lax.rem(q+k,ZC)*2,2)],r1.at[k],a1,k,zp(k))
    each(ZC,lambda k: ga(k).start())
    from_y=lax.rem(lax.div(q,2),Y)
    my=lambda k: rc(mall,mall,ms,k,yp(k))
    @pl.when(home)
    def _():
        zbuf[q]=tbuf[lax.div(q,8)*2+lax.rem(q,2)]
        def arrive(s,_):
            @pl.when(s!=q)
            def _(): rc(tbuf.at[0],zbuf.at[s],zs,s,(x*ZC+q,y)).wait_recv()
            return 0
        lax.fori_loop(0,ZC,arrive,0)
        for m in range(MB):
            acc=zbuf[0,m].astype(f32)
            for s in range(1,ZC): acc=acc+zbuf[s,m].astype(f32)
            mall[m]=acc.astype(bf16)
        each(Y,lambda k: my(k).start())
    each(ZC,lambda k: ga(k).wait())
    acc=g1[pl.ds(q*2,2)]
    for k in range(1,ZC): acc=acc+r1[k]
    x1[x]=acc
    gb=lambda k: rc(x1.at[x],x1.at[x],b1,k,xp(k))
    each(X,lambda k: gb(k).start())
    @pl.when(jnp.logical_not(home))
    def _(): my(lax.rem(y+Y-from_y,Y)).wait_recv()
    loads[1].wait()
    for m in range(MB):
        vdg=vdg+jnp.dot(mall[m],mem_ref[m*BLK:(m+1)*BLK,:],preferred_element_type=f32)
    split(g2,0,vdg)
    g2[14]=jnp.zeros((8,128),f32); g2[15]=jnp.zeros((8,128),f32)
    ha=lambda k: rc(g2.at[lax.rem(q+k,ZC)],r2.at[k],a2,k,zp(k))
    each(ZC,lambda k: ha(k).start())
    each(X,lambda k: gb(k).wait())
    o1[q]=x1[0]+x1[1]+x1[2]+x1[3]
    gd=lambda k: rc(o1.at[q],o1.at[q],d1,k,zp(k))
    each(ZC,lambda k: gd(k).start())
    each(ZC,lambda k: ha(k).wait())
    acc=g2[q]
    for k in range(1,ZC): acc=acc+r2[k]
    x2[x]=acc
    hb=lambda k: rc(x2.at[x],x2.at[x],b2,k,xp(k))
    each(X,lambda k: hb(k).start())
    each(X,lambda k: hb(k).wait())
    o2[q]=x2[0]+x2[1]+x2[2]+x2[3]
    hd=lambda k: rc(o2.at[q],o2.at[q],d2,k,zp(k))
    each(ZC,lambda k: hd(k).start())
    each(Y,lambda k: ly(k).wait())
    for s in range(Y):
        logit_out[:,s*BLK:(s+1)*BLK]=lall[s]
    for j in range(4):
        @pl.when(owner(j)!=q)
        def _(): pltpu.make_async_remote_copy(src_ref=tbuf.at[j],dst_ref=zbuf.at[q],send_sem=ys.at[0,j],recv_sem=zs.at[1,q],device_id=(x*ZC+owner(j),y),device_id_type=MESH).wait_send()
    @pl.when(home)
    def _(): each(Y,lambda k: my(k).wait_send())
    each(ZC,lambda k: gd(k).wait())
    for k in range(15):
        for i in range(2):
            grad_out[i*8:(i+1)*8,k*128:(k+1)*128]=o1[k,i]
    each(ZC,lambda k: hd(k).wait())
    for k in range(14):
        grad_out[(k%2)*8:(k%2)*8+8,(15+k//2)*128:(16+k//2)*128]=o2[k]

def reduce_all(w,cols,qug,vug,mcot,slab,mem):
    vm=pl.BlockSpec(memory_space=pltpu.VMEM)
    wide=qug.shape[1]
    V=pltpu.VMEM
    sem=lambda n: pltpu.SemaphoreType.DMA((2,n))
    return pl.pallas_call(reduce_kernel,
        in_specs=[pl.BlockSpec(memory_space=pltpu.SMEM)]+[vm]*4+[pl.BlockSpec(memory_space=pl.ANY)]*2,
        out_specs=[vm,vm],
        out_shape=[jax.ShapeDtypeStruct((TAGS,slab.shape[0]),f32),jax.ShapeDtypeStruct((RANK,3*wide+HD),f32)],
        scratch_shapes=[V(slab.shape,bf16),V(mem.shape,bf16),V((X*Y,4,RANK,BLK),bf16),V((4,MB,RANK,BLK),bf16),V((ZC,MB,RANK,BLK),bf16),V((MB,RANK,BLK),bf16),
            V((Y,TAGS+2*RANK,BLK),f32),V((Y,TAGS,BLK),f32),V((Y,2*RANK,BLK),bf16),
            V((32,8,128),f32),V((ZC,2,8,128),f32),V((X,2,8,128),f32),V((ZC,2,8,128),f32),
            V((16,8,128),f32),V((ZC,8,128),f32),V((X,8,128),f32),V((ZC,8,128),f32),
            sem(X*Y),sem(4),sem(ZC),sem(Y),sem(Y),sem(Y),sem(Y),sem(ZC),sem(X),sem(ZC),sem(ZC),sem(X),sem(ZC),pltpu.SemaphoreType.DMA((2,))],
        compiler_params=pltpu.CompilerParams(collective_id=1,has_side_effects=True,vmem_limit_bytes=60*2**20),
    )(w,cols,qug,vug,mcot,slab,mem)

UNITS=8
AHEAD=1
PLAN={(1, 0): [(0, 1)], (2, 0): [(1, 1), (0, 2)], (2, 1): [], (3, 0): [(2, 1), (1, 2), (0, 3)], (4, 0): [(3, 1), (2, 2), (1, 3), (0, 4)], (5, 0): [(3, 2), (2, 3), (1, 4), (0, 5)], (6, 0): [(3, 3), (2, 4), (1, 5)], (7, 0): [(3, 4), (2, 5)], (7, 1): [(3, 5)]}

def gather_kernel(mem_ref, slab_ref, wq_ref, wk_ref, wv_ref, qdown_hbm, vdown_hbm, qup_hbm, vup_hbm, ret_hbm,
                  pool, q_out, k_out, v_out, low_out, asked_out,
                  feat, wq, wkv, qdown_ref, vdown_ref, qup_ref, vup_ref, ret_ref, stage, mine, ysem, ssem, rsem, lsem, psem, osem, xsem):
    t=lax.axis_index("tm"); y=lax.axis_index("heads")
    x=lax.div(t,ZC); z=lax.rem(lax.div(t,2),Z); c=lax.rem(t,2)
    def tm(xx,zz,cc): return (xx*Z+zz)*2+cc
    xk=[lax.rem(x+k,X) for k in range(X)]
    devx=[(tm(xk[k],z,c),y) for k in range(X)]
    devz=[(tm(x,lax.rem(z+1,Z),c),y),(tm(x,lax.rem(z+Z-1,Z),c),y)]
    devc=(tm(x,z,1-c),y)
    devy=[(t,lax.rem(y+1,Y)),(t,lax.rem(y+Y-1,Y))]
    def rows_of(u):
        return (mem_ref if u<MB else slab_ref).at[pl.ds((u%MB)*BLK,BLK)]
    own=lambda u: pltpu.make_async_copy(rows_of(u),feat.at[u,y],osem.at[u])
    loads=[pltpu.make_async_copy(a,b,lsem.at[i]) for i,(a,b) in enumerate([(wk_ref,wkv.at[:,0:HD]),(wv_ref,wkv.at[:,HD:2*HD]),(vdown_hbm,vdown_ref),(vup_hbm,vup_ref),(ret_hbm,ret_ref),(wq_ref,wq),(qdown_hbm,qdown_ref),(qup_hbm,qup_ref)])]
    bar=pltpu.get_barrier_semaphore()
    for dev in devx[1:]+devz+devy+[devc]:
        pl.semaphore_signal(bar,inc=1,device_id=dev,device_id_type=MESH)
    for cp in loads: cp.start()
    for u in range(UNITS): own(u).start()
    mine[...]=jnp.zeros_like(mine)
    loads[4].wait()
    mine[0:MB,0:TOP]=ret_ref[...]
    pl.semaphore_wait(bar,X-1+5)

    def rc(src,dst,s,r,dev):
        return pltpu.make_async_remote_copy(src_ref=src,dst_ref=dst,send_sem=s,recv_sem=r,device_id=dev,device_id_type=MESH)
    left=lax.rem(y+Y-1,Y); right=lax.rem(y+1,Y)
    H=BLK//2
    def y_first(u): return [rc(rows_of(u),feat.at[u,y],ysem.at[0,u,i],ysem.at[1,u,i],devy[i]) for i in range(2)]
    def y_pass(u): return [rc(feat.at[u,left,pl.ds(0,H)],feat.at[u,left,pl.ds(0,H)],ysem.at[0,u,2],ysem.at[1,u,2],devy[0]),
                           rc(feat.at[u,right,pl.ds(H,H)],feat.at[u,right,pl.ds(H,H)],ysem.at[0,u,3],ysem.at[1,u,3],devy[1])]
    def start(cs):
        for cp in cs: cp.start()
    asked=lambda k: rc(mine,asked_out.at[k],xsem.at[0,k],xsem.at[1,k],devx[k])

    def part(b,cc,xs,zs): return pool.at[b,cc,xs,zs]
    every=pl.ds(0,X)
    GROUP=[pl.ds(0,1),pl.ds(1,2),pl.ds(3,2),pl.ds(5,2),pl.ds(7,1)]
    def share(b,cc,g): return rc(part(b,cc,every,GROUP[g]),part(b,cc,every,GROUP[g]),ssem.at[b,27+g],rsem.at[b,27+g],devc)
    def keep(b): return pltpu.make_async_copy(stage.at[b],pool.at[b,c,x,0],psem.at[b])
    def x_own(b,k): return rc(stage.at[b],pool.at[b,0,x,0],ssem.at[b,k-1],rsem.at[b,k],devx[k])
    def hop0(b,l,i):
        if l<3:
            src=0 if l==0 else 2*l-1+i
            return rc(part(b,0,every,src),part(b,0,every,2*l+1+i),ssem.at[b,3+2*l+i],rsem.at[b,4+2*l+i],devz[i])
        xs=pl.ds(2*i,2)
        return rc(part(b,0,xs,5+i),part(b,0,xs,7),ssem.at[b,9+i],rsem.at[b,10+i],devz[i])
    def core0(b,phase):
        if phase==1:
            for k in range(1,X): x_own(b,k).wait_recv()
            keep(b).wait()
            for i in range(2): hop0(b,0,i).start()
        else:
            l=phase-1
            for i in range(2):
                hop0(b,l-1,i).wait_recv()
                if l<4: hop0(b,l,i).start()
        share(b,0,phase-1).start()
    def hop1(b,l,i):
        src=stage.at[b] if l==0 else pool.at[b,1,x,2*l-1+i]
        return rc(src,pool.at[b,1,x,2*l+1+i if l<3 else 7],ssem.at[b,3+2*l+i if l<3 else 9],rsem.at[b,4+2*l+i if l<3 else 10],devz[i])
    def spread(b,g,k):
        src=part(b,1,x,GROUP[g])
        return rc(stage.at[pl.ds(b,1)] if g==0 else src,src,ssem.at[b,12+5*(k-1)+g],rsem.at[b,12+5*(k-1)+g],devx[k])
    def pass_on(b,g):
        for k in range(1,X): spread(b,g,k).wait_recv()
        share(b,1,g).start()
    def core1(b,phase):
        if phase<4:
            l=phase
            for i in range(2):
                hop1(b,l-1,i).wait_recv()
                if l<3 or b%2==i: hop1(b,l,i).start()
            for k in range(1,X): spread(b,l,k).start()
        elif phase==4:
            hop1(b,3,b%2).wait_recv()
            for k in range(1,X): spread(b,4,k).start()
        if phase==1: keep(b).wait()
        if phase in (2,3,4): pass_on(b,phase-2)
        if phase==5:
            pass_on(b,3); pass_on(b,4)
    def begin(b):
        keep(b).start()
        @pl.when(c==0)
        def _():
            for k in range(1,X): x_own(b,k).start()
        @pl.when(c==1)
        def _():
            for i in range(2): hop1(b,0,i).start()
            for k in range(1,X): spread(b,0,k).start()
    def step(b,phase):
        pl.when(c==0)(lambda: core0(b,phase))
        pl.when(c==1)(lambda: core1(b,phase))

    def project(u):
        own(u).wait()
        if u==0:
            for i in range(4): loads[i].wait()
        if u==MB:
            for i in range(5,8): loads[i].wait()
        memory=u<MB
        pair=jnp.zeros((BLK,2*HD),f32)
        low=jnp.zeros((RANK if memory else 2*RANK,BLK),f32)
        wide=wq.shape[1]
        for h in range(Y):
            cols=slice(h*wide,(h+1)*wide)
            piece=feat[u,h]
            pair=pair+jnp.dot(piece,wkv[cols,:],preferred_element_type=f32)
            down=vdown_ref[:,cols] if memory else jnp.concatenate([qdown_ref[:,cols],vdown_ref[:,cols]],axis=0)
            low=low+lax.dot_general(down,piece,NT,preferred_element_type=f32)
        low=low.astype(bf16)
        keys=pair[:,:HD].astype(bf16)
        values=(pair[:,HD:]+lax.dot_general(low[-RANK:],vup_ref[...],TN,preferred_element_type=f32)).astype(bf16)
        if memory:
            stage[u,0:BLK,:]=keys
            stage[u,BLK:2*BLK,:]=values
            stage[u,2*BLK:,:]=low
        else:
            b=u-MB
            rows=slice(b*BLK,(b+1)*BLK)
            k_out[rows,:]=keys
            v_out[rows,:]=values
            low_out[:,rows]=low
            acc=lax.dot_general(low[:RANK],qup_ref[...],TN,preferred_element_type=f32)
            for h in range(Y):
                acc=acc+jnp.dot(feat[u,h],wq[h*wide:(h+1)*wide,:],preferred_element_type=f32)
            q_out[rows,:]=acc.astype(bf16)

    for u in range(AHEAD): start(y_first(u))
    for k in range(1,X): asked(k).start()
    asked_out[0]=mine[...]
    for u in range(UNITS):
        for cp in y_first(u): cp.wait_recv()
        start(y_pass(u))
        if u+AHEAD<UNITS: start(y_first(u+AHEAD))
        for b,p in PLAN.get((u,0),[]): step(b,p)
        for cp in y_pass(u): cp.wait_recv()
        project(u)
        if u<MB: begin(u)
        for b,p in PLAN.get((u,1),[]): step(b,p)
    for k in range(1,X): asked(k).wait()
    for u in range(UNITS):
        for cp in y_first(u)+y_pass(u): cp.wait_send()
    for b in range(MB):
        for g in range(5):
            share(b,1-c,g).wait_recv()
            share(b,c,g).wait_send()
        @pl.when(c==0)
        def _():
            for k in range(1,X): x_own(b,k).wait_send()
            for l in range(4):
                for i in range(2): hop0(b,l,i).wait_send()
        @pl.when(c==1)
        def _():
            for l in range(3):
                for i in range(2): hop1(b,l,i).wait_send()
            hop1(b,3,b%2).wait_send()
            for g in range(5):
                for k in range(1,X): spread(b,g,k).wait_send()

def gather_all(mem,slab,wq,wk,wv,qdown,vdown,qup,vup,ret):
    vm=pl.BlockSpec(memory_space=pltpu.VMEM); hbm=pl.BlockSpec(memory_space=pl.ANY)
    n=slab.shape[0]; wide=wq.shape[1]
    S=jax.ShapeDtypeStruct; V=pltpu.VMEM; D=pltpu.SemaphoreType.DMA
    return pl.pallas_call(gather_kernel,
        in_specs=[hbm]*10,
        out_specs=[hbm]+[vm]*5,
        out_shape=[S((MB,2,X,Z,ROWS,HD),bf16),S((n,wide),bf16),S((n,HD),bf16),S((n,HD),bf16),S((2*RANK,n),bf16),S((X,8,128),jnp.int32)],
        scratch_shapes=[V((UNITS,Y,BLK,wide),bf16),V(wq.shape,bf16),V((wq.shape[0],2*HD),bf16),V(qdown.shape,bf16),V(vdown.shape,bf16),V(qup.shape,bf16),V(vup.shape,bf16),V(ret.shape,jnp.int32),
            V((MB,ROWS,HD),bf16),V((8,128),jnp.int32),
            D((2,UNITS,4)),D((MB,32)),D((MB,32)),D((8,)),D((MB,)),D((UNITS,)),D((2,X))],
        compiler_params=pltpu.CompilerParams(collective_id=2,has_side_effects=True,vmem_limit_bytes=60*2**20),
    )(mem,slab,wq,wk,wv,qdown,vdown,qup,vup,ret)

def local(slab_tokens,memory,query_weight,key_weight,value_weight,query_down,query_up,value_down,value_up,tag_weight,retrieval,boundary,grad_tags):
    x,y,q=place()
    pool,queries,keys,values,low_t,asked=gather_all(memory,slab_tokens,query_weight,key_weight,value_weight,query_down,value_down,query_up,value_up,retrieval)
    blocks=x*ZC*MB+jnp.arange(ZC*MB,dtype=jnp.int32)
    w=jnp.any(asked[:,:MB,:TOP].reshape(X,-1)[:,:,None]==blocks[None,None,:],axis=1).astype(f32)
    cols,qug,vug,mcot=attend(retrieval,boundary,queries,keys,values,low_t,grad_tags.T,tag_weight.T,query_up,value_up,pool)
    logits,grads=reduce_all(w,cols,qug,vug,mcot,slab_tokens,memory)
    wide=qug.shape[1]
    return logits.T,grads[:,:wide],grads[:,wide:2*wide],grads[:,2*wide+HD:],grads[:,2*wide:2*wide+HD]


def solution(mesh):
    in_specs=(P("tm","heads"),P("tm","heads"),P(None,"heads"),P(None,"heads"),P(None,"heads"),P(),P(None,"heads"),P(),P(None,"heads"),P("heads",None),P("tm",None),P("tm"),P("tm",None))
    out_specs=(P("tm",None),P(None,"heads"),P(None,"heads"),P(None,"heads"),P(None,"heads"))
    return jax.shard_map(local,mesh=mesh,in_specs=in_specs,out_specs=out_specs,check_vma=False)
```

time: 294 us -> 161 us (0.55)
  waiting for transfers between devices: 133 us -> 0 us
  Pallas kernels: 70.2 us -> 154 us
  blocking collectives: 51.2 us -> 0 us
  matrix products: 19.7 us -> 0 us
  between operations: 14.1 us -> 0.67 us
    all_gather x3 -> x0, waiting for transfers between devices: 132 us -> none  [the longest x1 81.7 us: local(): pool = lax.all_gather(piece, 'tm', axis=0, tiled=True)]
    pallas_call x0 -> x1, Pallas kernels: none -> 95.9 us  [gather_all(): pl.pallas_call(gather_kernel, in_specs=[hbm] * 10, out_specs=[hbm] + [vm]...]
    all_gather x1 -> x0, blocking collectives: 51.2 us -> none  [local(): lax.all_gather(retrieval, 'tm', axis=0, tiled=True).reshape(OWNERS, -1)]
    dot_general x8 -> x0, matrix products: 19.7 us -> none  [the longest x6 13.3 us: local(): dot = lambda a, b: jnp.dot(a, b, preferred_element_type=f32)]
    pallas_call x1, Pallas kernels: 46 us -> 36.9 us  [reduce_all(): pl.pallas_call(reduce_kernel, in_specs=[pl.BlockSpec(memory_space=pltpu.S...]
  transfers between devices with their start and end apart: 3 -> 0, of which waited for: 2 -> 0; matrix products, arithmetic and copies ran while one was open for 8% -> 0% of each run, Pallas kernels for 0% -> 0%
where the time goes in v3:
time: 161 us
  Pallas kernels  154 us (96%)
  local copies, waits for them, and re-layouts  4.96 us (3%)
    pallas_call x1, Pallas kernels, gather_all(): pl.pallas_call(gather_kernel, in_specs=[hbm] * 10, out_specs=[hbm] + [vm]...  95.9 us
    pallas_call x1, Pallas kernels, reduce_all(): pl.pallas_call(reduce_kernel, in_specs=[pl.BlockSpec(memory_space=pltpu.S...  36.9 us
    pallas_call x1, Pallas kernels, attend(): pl.pallas_call(attend_kernel, grid_spec=pltpu.PrefetchScalarGridSpec(num_...  21.6 us

profile of v3, /device:TPU:1, one launch (start us, length us, event | category | flops | bytes accessed | tf_op | source)
XLA Modules:
  0.0 160.7 jit_solution(12451763788633363726)
XLA Ops:
  0.6 95.9 %shard_map.164 = (bf16[4,2,4,8,272,128]{5,4,3,2,1,0:T(8,128)(2,1)}, bf16[512,896]{1,0:T(8,128)(2,1)}, bf16[512,128]{1,0:T(8,128)(2,1)}, bf16[512,128]{1,0:T(8,12...) custom-call(bf16[512,896]{1,0:T(8,128)(2,1)} %mem_hbm.1, bf16[512,896]{1,0:T(8,128)(2,1)} %slab_hbm.1, ...), custom_call_target="tpu_custom_call" | custom-call | tf_op jit(solution)/shard_map/pallas_call | solution.py:474
  96.5 0.7 slice.15
  97.3 0.1 eq.15
  97.3 0.1 compare_reduce_fusion
  97.4 0.6 convert_element_type.3.w_ref
  98.0 21.6 %shard_map.165 = (f32[4,40,128]{2,1,0:T(8,128)}, f32[16,896]{1,0:T(8,128)}, f32[16,128]{1,0:T(8,128)}, bf16[64,16,128]{2,1,0:T(8,128)(2,1)}) custom-call(s32[4,8]{1,0:T(4,128)} %ret.1, s32[4]{0:T(128)} %bnd.1, bf16[512,896]{1,0:T(8,128)(2,1)} %get-tuple-element.18.q_hbm, bf16[512,128]{1,0:T(8,128)(2,1)} %get-tuple-element.19.kl_hbm, ...), custom_call_target="tpu_custom_call" | custom-call | tf_op jit(solution)/shard_map/pallas_call | solution.py:137
  119.7 36.9 %shard_map.166 = (f32[8,512]{1,0:T(8,128)}, f32[16,2816]{1,0:T(8,128)}) custom-call(f32[4,64]{1,0:T(4,128)} %convert_element_type.3.w_ref, f32[4,40,128]{2,1,0:T(8,128)} %get-tuple-element.23.cols_ref, f32[16,896]{1,0:T(8,128)} %get-tuple-element.24.qug_ref, f32[16,128]{1,0:T(8,128)} %get-tuple-element.25.vug_ref, ...), custom_call_target="tpu_custom_call" | custom-call | tf_op jit(solution)/shard_map/pallas_call | solution.py:293
  156.6 1.3 slice.19
  157.9 1.5 fusion
  159.4 1.3 copy.19
  (1 shorter events, 0.0 us)

commit v4 on v3

--- a/solution.py
+++ b/solution.py
@@ -62,57 +62,62 @@
     vv[own,:]=vl_ref[rows,:]
     lt[:,own]=low_ref[RANK:,rows]
     edge=bnd[c]
-    m=jnp.full((1,wide),-jnp.inf,f32)
     scale=HD**-0.5
     n_ch=nkeys//CH
+    split=(heads+1)//2*HD
+    groups=[slice(0,split),slice(split,wide)]
+    span=[slice(j*CH,(j+1)*CH) for j in range(n_ch)]
+    key=lax.broadcasted_iota(jnp.int32,(BLK,BLK),0)
+    row=lax.broadcasted_iota(jnp.int32,(BLK,BLK),1)
+    seen=(key<=row)&((key>=edge)|(row<edge))
+    bias=jnp.where(seen,0.0,-jnp.inf).astype(f32)
+    most=[jnp.full((1,g.stop-g.start),-jnp.inf,f32) for g in groups]
+    total=[jnp.zeros((1,g.stop-g.start),f32) for g in groups]
+    out=[jnp.zeros((HD,g.stop-g.start),f32) for g in groups]
+    back=[jnp.zeros((HD,g.stop-g.start),f32) for g in groups]
+    inv=[None,None]; dots=[None,None]
+    def scores(n,j):
+        g=groups[n]
+        s=lax.dot_general(kk[span[j],:],qs[g,:],NT,preferred_element_type=f32)
+        if j==n_ch-1:
+            last=s[CH-BLK:]+jnp.concatenate([bias]*((g.stop-g.start)//BLK),axis=1)
+            s=jnp.concatenate([s[:CH-BLK],last],axis=0)
+        st[span[j],g]=s
+        most[n]=jnp.maximum(most[n],jnp.max(s,axis=0,keepdims=True))
+    def expo(n,j):
+        e=jnp.exp2((st[span[j],groups[n]]-most[n])*(scale*LOG2E))
+        st[span[j],groups[n]]=e
+        total[n]=total[n]+jnp.sum(e,axis=0,keepdims=True)
+    def attended(n,j):
+        if j==0: inv[n]=1.0/total[n]
+        low=(st[span[j],groups[n]]*inv[n]).astype(bf16)
+        pb[span[j],groups[n]]=low
+        out[n]=out[n]+lax.dot_general(vv[span[j],:],low,TN,preferred_element_type=f32)
+    def backward(n,j):
+        g=groups[n]
+        if j==0:
+            low=out[n].astype(bf16)
+            for h in range(g.start//HD,g.stop//HD):
+                at[h*HD:(h+1)*HD,:]=low[:,h*HD-g.start:(h+1)*HD-g.start]
+            dots[n]=jnp.sum(gm[:,g].astype(f32)*low.astype(f32),axis=0,keepdims=True)
+            inv[n]=inv[n]*scale
+        pg=jnp.dot(vv[span[j],:],gm[:,g],preferred_element_type=f32)
+        sg=((st[span[j],g]*inv[n])*(pg-dots[n])).astype(bf16)
+        back[n]=back[n]+lax.dot_general(kk[span[j],:],sg,TN,preferred_element_type=f32)
+        if j==n_ch-1:
+            low=back[n].astype(bf16)
+            for h in range(g.start//HD,g.stop//HD):
+                qg[h*HD:(h+1)*HD,:]=low[:,h*HD-g.start:(h+1)*HD-g.start]
+    for j in range(n_ch): scores(0,j)
+    for j in range(n_ch): scores(1,j); expo(0,j)
+    for j in range(n_ch): attended(0,j); expo(1,j)
+    for j in range(n_ch): attended(1,j); backward(0,j)
     for j in range(n_ch):
-        r=slice(j*CH,(j+1)*CH)
-        s=lax.dot_general(kk[r,:],qs[...],NT,preferred_element_type=f32)
-        if j==n_ch-1:
-            key=lax.broadcasted_iota(jnp.int32,(BLK,BLK),0)
-            row=lax.broadcasted_iota(jnp.int32,(BLK,BLK),1)
-            seen=(key<=row)&((key>=edge)|(row<edge))
-            bias=jnp.where(seen,0.0,-jnp.inf).astype(f32)
-            bias=jnp.concatenate([bias]*heads,axis=1)
-            last=s[CH-BLK:]+bias
-            s=jnp.concatenate([s[:CH-BLK],last],axis=0)
-        st[r,:]=s
-        m=jnp.maximum(m,jnp.max(s,axis=0,keepdims=True))
-    tot=jnp.zeros((1,wide),f32)
-    for j in range(n_ch):
-        r=slice(j*CH,(j+1)*CH)
-        e=jnp.exp2((st[r,:]-m)*(scale*LOG2E))
-        st[r,:]=e
-        tot=tot+jnp.sum(e,axis=0,keepdims=True)
-    inv=1.0/tot
-    acc=jnp.zeros((HD,wide),f32)
-    for j in range(n_ch):
-        r=slice(j*CH,(j+1)*CH)
-        pl_=(st[r,:]*inv).astype(bf16)
-        pb[r,:]=pl_
-        acc=acc+lax.dot_general(vv[r,:],pl_,TN,preferred_element_type=f32)
-    att=acc.astype(bf16)
-    at[...]=att
-    dot_row=jnp.sum(gm[...].astype(f32)*att.astype(f32),axis=0,keepdims=True)
-    inv=inv*scale
-    acc=jnp.zeros((HD,wide),f32)
-    for j in range(n_ch):
-        r=slice(j*CH,(j+1)*CH)
-        pg=jnp.dot(vv[r,:],gm[...],preferred_element_type=f32)
-        sgr=((st[r,:]*inv)*(pg-dot_row)).astype(bf16)
-        acc=acc+lax.dot_general(kk[r,:],sgr,TN,preferred_element_type=f32)
-        vg[r,:]=jnp.dot(pb[r,:],gs[...],preferred_element_type=f32)
-    qg[...]=acc.astype(bf16)
-    logits=jnp.zeros((TAGS,BLK),f32)
-    qcot=jnp.zeros((RANK,BLK),f32)
-    for h in range(heads):
-        cols=slice(h*HD,(h+1)*HD)
-        qgh=qg[:,cols]
-        logits=logits+jnp.dot(twt_ref[:,cols],at[:,cols],preferred_element_type=f32)
-        qcot=qcot+jnp.dot(qup_ref[:,cols],qgh,preferred_element_type=f32)
-        qug_ref[:,cols]+=lax.dot_general(low_ref[:RANK,rows],qgh,NT,preferred_element_type=f32)
-    cols_ref[c,0:TAGS,:]=logits
-    cols_ref[c,TAGS:TAGS+RANK,:]=qcot
+        backward(1,j)
+        vg[span[j],:]=jnp.dot(pb[span[j],:],gs[...],preferred_element_type=f32)
+    cols_ref[c,0:TAGS,:]=jnp.dot(twt_ref[...],at[...],preferred_element_type=f32)
+    cols_ref[c,TAGS:TAGS+RANK,:]=jnp.dot(qup_ref[...],qg[...],preferred_element_type=f32)
+    qug_ref[...]+=lax.dot_general(low_ref[:RANK,rows],qg[...],NT,preferred_element_type=f32)
     whole=vg[...]
     high=whole.astype(bf16)
     rest=(whole-high.astype(f32)).astype(bf16)
@@ -142,7 +147,7 @@
               V((spans*TOP,ROWS,HD),bf16),V((nk,HD),bf16),V((nk,HD),bf16),V((RANK,nk),bf16),
               V((wide,HD),bf16),V((HD,wide),bf16),V((wide,HD),bf16),
               V((nk,wide),f32),V((nk,wide),bf16),
-              V((HD,wide),bf16),V((HD,wide),bf16),V((nk,HD),f32),V((OWNERS,RANK,BLK),f32),
+              V((wide,BLK),bf16),V((wide,BLK),bf16),V((nk,HD),f32),V((OWNERS,RANK,BLK),f32),
               pltpu.SemaphoreType.DMA((spans*TOP,)),pltpu.SemaphoreType.DMA((8,))]),
         out_shape=[shp(spans,TAGS+2*RANK,BLK),shp(RANK,wide),shp(RANK,HD),jax.ShapeDtypeStruct((OWNERS,RANK,BLK),bf16)],
         compiler_params=pltpu.CompilerParams(vmem_limit_bytes=60*2**20,dimension_semantics=("arbitrary",)),
@@ -152,9 +157,9 @@
     t=lax.axis_index("tm"); y=lax.axis_index("heads")
     return lax.div(t,ZC), y, lax.rem(t,ZC)
 
-def reduce_kernel(w_ref, cols_ref, qug_ref, vug_ref, mcot_ref, slab_hbm, mem_hbm,
+def reduce_kernel(asked_hbm, cols_hbm, qug_hbm, vug_hbm, mcot_hbm, slab_hbm, mem_hbm,
                   logit_out, grad_out,
-                  slab_ref, mem_ref, xbuf, tbuf, zbuf, mall, cbuf, lall, call, g1, r1, x1, o1, g2, r2, x2, o2,
+                  asked_ref, cols_ref, qug_ref, vug_ref, mcot_ref, slab_ref, mem_ref, wbuf, xbuf, tbuf, zbuf, mall, cbuf, lall, call, g1, r1, x1, o1, g2, r2, x2, o2,
                   xs, ys, zs, ms, cs, ls, ks, a1, b1, d1, a2, b2, d2, lsem):
     x,y,q=place()
     def xp(k): return (lax.rem(x+k,X)*ZC+q, y)
@@ -167,17 +172,27 @@
         lax.fori_loop(1,n,body,0)
     def rc(src,dst,sems,k,dev):
         return pltpu.make_async_remote_copy(src_ref=src,dst_ref=dst,send_sem=sems.at[0,k],recv_sem=sems.at[1,k],device_id=dev,device_id_type=MESH)
-    loads=[pltpu.make_async_copy(slab_hbm,slab_ref,lsem.at[0]),pltpu.make_async_copy(mem_hbm,mem_ref,lsem.at[1])]
+    loads=[pltpu.make_async_copy(a,b,lsem.at[i]) for i,(a,b) in enumerate([(mcot_hbm,mcot_ref),(cols_hbm,cols_ref),(asked_hbm,asked_ref),(slab_hbm,slab_ref),(qug_hbm,qug_ref),(vug_hbm,vug_ref),(mem_hbm,mem_ref)])]
     for cp in loads: cp.start()
     bar=pltpu.get_barrier_semaphore()
     each(X*Y,lambda k: pl.semaphore_signal(bar,inc=1,device_id=xyp(k),device_id_type=MESH))
     each(ZC,lambda k: pl.semaphore_signal(bar,inc=1,device_id=zp(k),device_id_type=MESH))
+    for i in range(2): loads[i].wait()
     pl.semaphore_wait(bar,X*Y+ZC-2)
     def slots(k): return pl.ds(lax.rem(x+lax.div(k,Y),X)*ZC+lax.rem(y+lax.rem(k,Y),Y)*4,4)
     mx=lambda k: rc(mcot_ref.at[slots(k)],xbuf.at[k],xs,k,xyp(k))
     cy=lambda k: rc(cols_ref.at[lax.rem(y+k,Y)],cbuf.at[k],cs,k,yp(k))
     each(X*Y,lambda k: mx(k).start())
     each(Y,lambda k: cy(k).start())
+    def owner(j):
+        half,core=(j//2,j%2) if isinstance(j,int) else (lax.div(j,2),lax.rem(j,2))
+        return (y+Y*half)*2+core
+    loads[2].wait()
+    for j in range(4):
+        for m in range(MB):
+            for k in range(X):
+                hit=jnp.where(asked_ref[k]==(x*ZC+owner(j))*MB+m,1.0,0.0).astype(f32)
+                wbuf[j,m,k:k+1,:]=jnp.broadcast_to(jnp.max(jnp.max(hit,axis=0,keepdims=True),axis=1,keepdims=True),(1,128))
     each(Y,lambda k: cy(k).wait())
     total=cols_ref[y]+cbuf[1]+cbuf[2]+cbuf[3]
     lall[y]=total[:TAGS]
@@ -188,9 +203,6 @@
     each(Y,lambda k: ly(k).start())
     xbuf[0]=mcot_ref[slots(0)]
     each(X*Y,lambda k: mx(k).wait())
-    def owner(j):
-        half,core=(j//2,j%2) if isinstance(j,int) else (lax.div(j,2),lax.rem(j,2))
-        return (y+Y*half)*2+core
     def expand(j,_):
         parts=[]
         for k in range(X):
@@ -198,10 +210,9 @@
             for i in range(1,Y): s=s+xbuf[Y*k+i,j].astype(f32)
             parts.append(s)
         for m in range(MB):
-            at=owner(j)*MB+m
-            acc=parts[0]*w_ref[0,at]
+            acc=parts[0]*wbuf[j,m,0:1,:]
             for k in range(1,X):
-                acc=acc+parts[k]*w_ref[k,at]
+                acc=acc+parts[k]*wbuf[j,m,k:k+1,:]
             tbuf[j,m]=acc.astype(bf16)
         return 0
     lax.fori_loop(0,4,expand,0)
@@ -216,7 +227,7 @@
             ref[first+2*j]=value[0:8,j*128:(j+1)*128]
             ref[first+2*j+1]=value[8:16,j*128:(j+1)*128]
     qdg=jnp.zeros(qug_ref.shape,f32); vdg=jnp.zeros(qug_ref.shape,f32)
-    loads[0].wait()
+    for i in range(3,6): loads[i].wait()
     for s in range(Y):
         piece=slab_ref[s*BLK:(s+1)*BLK,:]
         qdg=qdg+jnp.dot(call[s,0:RANK],piece,preferred_element_type=f32)
@@ -248,7 +259,7 @@
     each(X,lambda k: gb(k).start())
     @pl.when(jnp.logical_not(home))
     def _(): my(lax.rem(y+Y-from_y,Y)).wait_recv()
-    loads[1].wait()
+    loads[6].wait()
     for m in range(MB):
         vdg=vdg+jnp.dot(mall[m],mem_ref[m*BLK:(m+1)*BLK,:],preferred_element_type=f32)
     split(g2,0,vdg)
@@ -285,25 +296,40 @@
     for k in range(14):
         grad_out[(k%2)*8:(k%2)*8+8,(15+k//2)*128:(16+k//2)*128]=o2[k]
 
-def reduce_all(w,cols,qug,vug,mcot,slab,mem):
+def reduce_all(asked,cols,qug,vug,mcot,slab,mem):
     vm=pl.BlockSpec(memory_space=pltpu.VMEM)
     wide=qug.shape[1]
     V=pltpu.VMEM
     sem=lambda n: pltpu.SemaphoreType.DMA((2,n))
     return pl.pallas_call(reduce_kernel,
-        in_specs=[pl.BlockSpec(memory_space=pltpu.SMEM)]+[vm]*4+[pl.BlockSpec(memory_space=pl.ANY)]*2,
+        in_specs=[pl.BlockSpec(memory_space=pl.ANY)]*7,
         out_specs=[vm,vm],
         out_shape=[jax.ShapeDtypeStruct((TAGS,slab.shape[0]),f32),jax.ShapeDtypeStruct((RANK,3*wide+HD),f32)],
-        scratch_shapes=[V(slab.shape,bf16),V(mem.shape,bf16),V((X*Y,4,RANK,BLK),bf16),V((4,MB,RANK,BLK),bf16),V((ZC,MB,RANK,BLK),bf16),V((MB,RANK,BLK),bf16),
+        scratch_shapes=[V(a.shape,a.dtype) for a in (asked,cols,qug,vug,mcot,slab,mem)]+[V((4,MB,8,128),f32),V((X*Y,4,RANK,BLK),bf16),V((4,MB,RANK,BLK),bf16),V((ZC,MB,RANK,BLK),bf16),V((MB,RANK,BLK),bf16),
             V((Y,TAGS+2*RANK,BLK),f32),V((Y,TAGS,BLK),f32),V((Y,2*RANK,BLK),bf16),
             V((32,8,128),f32),V((ZC,2,8,128),f32),V((X,2,8,128),f32),V((ZC,2,8,128),f32),
             V((16,8,128),f32),V((ZC,8,128),f32),V((X,8,128),f32),V((ZC,8,128),f32),
-            sem(X*Y),sem(4),sem(ZC),sem(Y),sem(Y),sem(Y),sem(Y),sem(ZC),sem(X),sem(ZC),sem(ZC),sem(X),sem(ZC),pltpu.SemaphoreType.DMA((2,))],
+            sem(X*Y),sem(4),sem(ZC),sem(Y),sem(Y),sem(Y),sem(Y),sem(ZC),sem(X),sem(ZC),sem(ZC),sem(X),sem(ZC),pltpu.SemaphoreType.DMA((7,))],
         compiler_params=pltpu.CompilerParams(collective_id=1,has_side_effects=True,vmem_limit_bytes=60*2**20),
-    )(w,cols,qug,vug,mcot,slab,mem)
+    )(asked,cols,qug,vug,mcot,slab,mem)
+
+def unpack_kernel(logits, grads, a, b, c, d, e, sems):
+    wide=b.shape[1]
+    jobs=[(logits,a),(grads.at[:,0:wide],b),(grads.at[:,wide:2*wide],c),(grads.at[:,2*wide+HD:],d),(grads.at[:,2*wide:2*wide+HD],e)]
+    copies=[pltpu.make_async_copy(s,t,sems.at[i]) for i,(s,t) in enumerate(jobs)]
+    for cp in copies: cp.start()
+    for cp in copies: cp.wait()
+
+def unpack(logits,grads,wide):
+    S=jax.ShapeDtypeStruct; hbm=pl.BlockSpec(memory_space=pl.ANY)
+    return pl.pallas_call(unpack_kernel,in_specs=[hbm]*2,out_specs=[hbm]*5,
+        out_shape=[S(logits.shape,f32)]+[S((RANK,wide),f32)]*3+[S((RANK,HD),f32)],
+        scratch_shapes=[pltpu.SemaphoreType.DMA((5,))],
+        compiler_params=pltpu.CompilerParams(vmem_limit_bytes=60*2**20))(logits,grads)
 
 UNITS=8
-AHEAD=1
+FIRST={-1: [0], 0: [1], 1: [2], 2: [3], 3: [4], 4: [5], 5: [6], 6: [7]}
+LATE=1
 PLAN={(1, 0): [(0, 1)], (2, 0): [(1, 1), (0, 2)], (2, 1): [], (3, 0): [(2, 1), (1, 2), (0, 3)], (4, 0): [(3, 1), (2, 2), (1, 3), (0, 4)], (5, 0): [(3, 2), (2, 3), (1, 4), (0, 5)], (6, 0): [(3, 3), (2, 4), (1, 5)], (7, 0): [(3, 4), (2, 5)], (7, 1): [(3, 5)]}
 
 def gather_kernel(mem_ref, slab_ref, wq_ref, wk_ref, wv_ref, qdown_hbm, vdown_hbm, qup_hbm, vup_hbm, ret_hbm,
@@ -324,11 +350,7 @@
     bar=pltpu.get_barrier_semaphore()
     for dev in devx[1:]+devz+devy+[devc]:
         pl.semaphore_signal(bar,inc=1,device_id=dev,device_id_type=MESH)
-    for cp in loads: cp.start()
-    for u in range(UNITS): own(u).start()
-    mine[...]=jnp.zeros_like(mine)
-    loads[4].wait()
-    mine[0:MB,0:TOP]=ret_ref[...]
+    for cp in loads[:4]: cp.start()
     pl.semaphore_wait(bar,X-1+5)
 
     def rc(src,dst,s,r,dev):
@@ -345,25 +367,32 @@
     def part(b,cc,xs,zs): return pool.at[b,cc,xs,zs]
     every=pl.ds(0,X)
     GROUP=[pl.ds(0,1),pl.ds(1,2),pl.ds(3,2),pl.ds(5,2),pl.ds(7,1)]
-    def share(b,cc,g): return rc(part(b,cc,every,GROUP[g]),part(b,cc,every,GROUP[g]),ssem.at[b,27+g],rsem.at[b,27+g],devc)
+    def share(b,cc,g): return rc(part(b,cc,every,GROUP[g]),part(b,cc,every,GROUP[g]),ssem.at[b,32+g],rsem.at[b,32+g],devc)
     def keep(b): return pltpu.make_async_copy(stage.at[b],pool.at[b,c,x,0],psem.at[b])
     def x_own(b,k): return rc(stage.at[b],pool.at[b,0,x,0],ssem.at[b,k-1],rsem.at[b,k],devx[k])
-    def hop0(b,l,i):
-        if l<3:
-            src=0 if l==0 else 2*l-1+i
-            return rc(part(b,0,every,src),part(b,0,every,2*l+1+i),ssem.at[b,3+2*l+i],rsem.at[b,4+2*l+i],devz[i])
-        xs=pl.ds(2*i,2)
-        return rc(part(b,0,xs,5+i),part(b,0,xs,7),ssem.at[b,9+i],rsem.at[b,10+i],devz[i])
+    back=[x]+[lax.rem(x+X-k,X) for k in range(1,X)]
+    def hop0(b,l,i,k):
+        src=part(b,0,back[k],0 if l==0 else 2*l-1+i)
+        return rc(stage.at[b] if l==0 and k==0 else src,part(b,0,back[k],2*l+1+i),ssem.at[b,3+8*l+2*k+i],rsem.at[b,4+8*l+2*k+i],devz[i])
+    def last0(b,k):
+        low=back[k]<X//2
+        dev=(jnp.where(low,devz[0][0],devz[1][0]),y)
+        return rc(part(b,0,back[k],jnp.where(low,5,6)),part(b,0,back[k],7),ssem.at[b,27+k],rsem.at[b,28+k],dev)
     def core0(b,phase):
         if phase==1:
-            for k in range(1,X): x_own(b,k).wait_recv()
+            for k in range(1,X):
+                x_own(b,k).wait_recv()
+                for i in range(2): hop0(b,0,i,k).start()
             keep(b).wait()
-            for i in range(2): hop0(b,0,i).start()
+        elif phase<5:
+            l=phase-1
+            for k in range(X):
+                for i in range(2):
+                    hop0(b,l-1,i,k).wait_recv()
+                    if l<3: hop0(b,l,i,k).start()
+                if l==3: last0(b,k).start()
         else:
-            l=phase-1
-            for i in range(2):
-                hop0(b,l-1,i).wait_recv()
-                if l<4: hop0(b,l,i).start()
+            for k in range(X): last0(b,k).wait_recv()
         share(b,0,phase-1).start()
     def hop1(b,l,i):
         src=stage.at[b] if l==0 else pool.at[b,1,x,2*l-1+i]
@@ -392,6 +421,7 @@
         keep(b).start()
         @pl.when(c==0)
         def _():
+            for i in range(2): hop0(b,0,i,0).start()
             for k in range(1,X): x_own(b,k).start()
         @pl.when(c==1)
         def _():
@@ -435,18 +465,25 @@
                 acc=acc+jnp.dot(feat[u,h],wq[h*wide:(h+1)*wide,:],preferred_element_type=f32)
             q_out[rows,:]=acc.astype(bf16)
 
-    for u in range(AHEAD): start(y_first(u))
+    for v in FIRST[-1]: start(y_first(v))
+    for u in range(UNITS): own(u).start()
+    for cp in loads[4:]: cp.start()
+    mine[...]=jnp.full(mine.shape,-1,jnp.int32)
+    loads[4].wait()
+    mine[0:MB,0:TOP]=ret_ref[...]
     for k in range(1,X): asked(k).start()
     asked_out[0]=mine[...]
     for u in range(UNITS):
         for cp in y_first(u): cp.wait_recv()
         start(y_pass(u))
-        if u+AHEAD<UNITS: start(y_first(u+AHEAD))
+        for v in FIRST.get(u,[]): start(y_first(v))
+        if LATE and u>MB: project(u-1)
         for b,p in PLAN.get((u,0),[]): step(b,p)
         for cp in y_pass(u): cp.wait_recv()
-        project(u)
+        if u<MB or not LATE: project(u)
         if u<MB: begin(u)
         for b,p in PLAN.get((u,1),[]): step(b,p)
+    if LATE: project(UNITS-1)
     for k in range(1,X): asked(k).wait()
     for u in range(UNITS):
         for cp in y_first(u)+y_pass(u): cp.wait_send()
@@ -457,8 +494,10 @@
         @pl.when(c==0)
         def _():
             for k in range(1,X): x_own(b,k).wait_send()
-            for l in range(4):
-                for i in range(2): hop0(b,l,i).wait_send()
+            for k in range(X):
+                for l in range(3):
+                    for i in range(2): hop0(b,l,i,k).wait_send()
+                last0(b,k).wait_send()
         @pl.when(c==1)
         def _():
             for l in range(3):
@@ -477,19 +516,16 @@
         out_shape=[S((MB,2,X,Z,ROWS,HD),bf16),S((n,wide),bf16),S((n,HD),bf16),S((n,HD),bf16),S((2*RANK,n),bf16),S((X,8,128),jnp.int32)],
         scratch_shapes=[V((UNITS,Y,BLK,wide),bf16),V(wq.shape,bf16),V((wq.shape[0],2*HD),bf16),V(qdown.shape,bf16),V(vdown.shape,bf16),V(qup.shape,bf16),V(vup.shape,bf16),V(ret.shape,jnp.int32),
             V((MB,ROWS,HD),bf16),V((8,128),jnp.int32),
-            D((2,UNITS,4)),D((MB,32)),D((MB,32)),D((8,)),D((MB,)),D((UNITS,)),D((2,X))],
+            D((2,UNITS,4)),D((MB,37)),D((MB,37)),D((8,)),D((MB,)),D((UNITS,)),D((2,X))],
         compiler_params=pltpu.CompilerParams(collective_id=2,has_side_effects=True,vmem_limit_bytes=60*2**20),
     )(mem,slab,wq,wk,wv,qdown,vdown,qup,vup,ret)
 
 def local(slab_tokens,memory,query_weight,key_weight,value_weight,query_down,query_up,value_down,value_up,tag_weight,retrieval,boundary,grad_tags):
-    x,y,q=place()
     pool,queries,keys,values,low_t,asked=gather_all(memory,slab_tokens,query_weight,key_weight,value_weight,query_down,value_down,query_up,value_up,retrieval)
-    blocks=x*ZC*MB+jnp.arange(ZC*MB,dtype=jnp.int32)
-    w=jnp.any(asked[:,:MB,:TOP].reshape(X,-1)[:,:,None]==blocks[None,None,:],axis=1).astype(f32)
     cols,qug,vug,mcot=attend(retrieval,boundary,queries,keys,values,low_t,grad_tags.T,tag_weight.T,query_up,value_up,pool)
-    logits,grads=reduce_all(w,cols,qug,vug,mcot,slab_tokens,memory)
-    wide=qug.shape[1]
-    return logits.T,grads[:,:wide],grads[:,wide:2*wide],grads[:,2*wide+HD:],grads[:,2*wide:2*wide+HD]
+    logits,grads=reduce_all(asked,cols,qug,vug,mcot,slab_tokens,memory)
+    logits,a,b,c,d=unpack(logits,grads,qug.shape[1])
+    return logits.T,a,b,c,d
 
 
 def solution(mesh):

time: 161 us -> 158 us (0.981)
  local copies, waits for them, and re-layouts: 4.96 us -> 0 us
  Pallas kernels: 154 us -> 157 us
    pallas_call x1 -> x2, Pallas kernels: 36.9 us -> 42.7 us  [the longest x1 35.6 us: reduce_all(): pl.pallas_call(reduce_kernel, in_specs=[pl.BlockSpec(memory_space=pl.ANY)...]
    slice x3 -> x0, local copies, waits for them, and re-layouts: 3.56 us -> none  [the longest x1 1.54 us: local(): grads[:, 2 * wide + HD:]]
    pallas_call x1, Pallas kernels: 95.9 us -> 93.2 us  [gather_all(): pl.pallas_call(gather_kernel, in_specs=[hbm] * 10, out_specs=[hbm] + [vm]...]
where the time goes in v4:
time: 158 us
  Pallas kernels  157 us (99%)
    pallas_call x1, Pallas kernels, gather_all(): pl.pallas_call(gather_kernel, in_specs=[hbm] * 10, out_specs=[hbm] + [vm]...  93.2 us
    pallas_call x1, Pallas kernels, reduce_all(): pl.pallas_call(reduce_kernel, in_specs=[pl.BlockSpec(memory_space=pl.ANY)...  35.6 us
    pallas_call x1, Pallas kernels, attend(): pl.pallas_call(attend_kernel, grid_spec=pltpu.PrefetchScalarGridSpec(num_...  21.4 us
    pallas_call x1, Pallas kernels, unpack(): pl.pallas_call(unpack_kernel, in_specs=[hbm] * 2, out_specs=[hbm] * 5, ou...  7.11 us

profile of v4, /device:TPU:1, one launch (start us, length us, event | category | flops | bytes accessed | tf_op | source)
XLA Modules:
  0.0 158.1 jit_solution(17575907391678356655)
XLA Ops:
  0.6 93.2 %shard_map.164 = (bf16[4,2,4,8,272,128]{5,4,3,2,1,0:T(8,128)(2,1)}, bf16[512,896]{1,0:T(8,128)(2,1)}, bf16[512,128]{1,0:T(8,128)(2,1)}, bf16[512,128]{1,0:T(8,12...) custom-call(bf16[512,896]{1,0:T(8,128)(2,1)} %mem_hbm.1, bf16[512,896]{1,0:T(8,128)(2,1)} %slab_hbm.1, ...), custom_call_target="tpu_custom_call" | custom-call | tf_op jit(solution)/shard_map/pallas_call | solution.py:513
  93.8 21.4 %shard_map.165 = (f32[4,40,128]{2,1,0:T(8,128)}, f32[16,896]{1,0:T(8,128)}, f32[16,128]{1,0:T(8,128)}, bf16[64,16,128]{2,1,0:T(8,128)(2,1)}) custom-call(s32[4,8]{1,0:T(4,128)} %ret.1, s32[4]{0:T(128)} %bnd.1, bf16[512,896]{1,0:T(8,128)(2,1)} %get-tuple-element.23.q_hbm, bf16[512,128]{1,0:T(8,128)(2,1)} %get-tuple-element.24.kl_hbm, ...), custom_call_target="tpu_custom_call" | custom-call | tf_op jit(solution)/shard_map/pallas_call | solution.py:142
  115.2 35.6 %shard_map.166 = (f32[8,512]{1,0:T(8,128)}, f32[16,2816]{1,0:T(8,128)}) custom-call(s32[4,8,128]{2,1,0:T(8,128)} %get-tuple-element.22.asked_hbm, f32[4,40,128]{2,1,0:T(8,128)} %get-tuple-element.28.cols_hbm, f32[16,896]{1,0:T(8,128)} %get-tuple-element.29.qug_hbm, f32[16,128]{1,0:T(8,128)} %get-tuple-element.30.vug_hbm, ...), custom_call_target="tpu_custom_call" | custom-call | tf_op jit(solution)/shard_map/pallas_call | solution.py:304
  150.9 7.1 %shard_map.167 = (f32[8,512]{1,0:T(8,128)}, f32[16,896]{1,0:T(8,128)}, f32[16,896]{1,0:T(8,128)}, f32[16,896]{1,0:T(8,128)}, f32[16,128]{1,0:T(8,128)}) custom-call(f32[8,512]{1,0:T(8,128)} %get-tuple-element.32.logits, f32[16,2816]{1,0:T(8,128)} %get-tuple-element.33.grads), custom_call_target="tpu_custom_call" | custom-call | tf_op jit(solution)/shard_map/pallas_call | solution.py:325

commit v5 on v4

--- a/solution.py
+++ b/solution.py
@@ -54,8 +54,10 @@
     for s in range(TOP):
         i=c*TOP+s
         fetch(i).wait()
-        kk[s*BLK:(s+1)*BLK,:]=land[i,0:128,:]
-        vv[s*BLK:(s+1)*BLK,:]=land[i,128:256,:]
+        for half in range(2):
+            dst=slice(s*BLK+half*64,s*BLK+half*64+64)
+            kk[dst,:]=land[i,half*128:half*128+64,:]
+            vv[dst,:]=land[i,half*128+64:half*128+128,:]
         lt[:,s*BLK:(s+1)*BLK]=land[i,256:272,:]
     own=slice(TOP*BLK,nkeys)
     kk[own,:]=kl_ref[rows,:]
@@ -313,24 +315,25 @@
         compiler_params=pltpu.CompilerParams(collective_id=1,has_side_effects=True,vmem_limit_bytes=60*2**20),
     )(asked,cols,qug,vug,mcot,slab,mem)
 
-def unpack_kernel(logits, grads, a, b, c, d, e, sems):
+def unpack_kernel(logits, grads, a, b, c, d, e):
     wide=b.shape[1]
-    jobs=[(logits,a),(grads.at[:,0:wide],b),(grads.at[:,wide:2*wide],c),(grads.at[:,2*wide+HD:],d),(grads.at[:,2*wide:2*wide+HD],e)]
-    copies=[pltpu.make_async_copy(s,t,sems.at[i]) for i,(s,t) in enumerate(jobs)]
-    for cp in copies: cp.start()
-    for cp in copies: cp.wait()
+    a[...]=logits[...]
+    b[...]=grads[:,0:wide]
+    c[...]=grads[:,wide:2*wide]
+    d[...]=grads[:,2*wide+HD:]
+    e[...]=grads[:,2*wide:2*wide+HD]
 
 def unpack(logits,grads,wide):
-    S=jax.ShapeDtypeStruct; hbm=pl.BlockSpec(memory_space=pl.ANY)
-    return pl.pallas_call(unpack_kernel,in_specs=[hbm]*2,out_specs=[hbm]*5,
+    S=jax.ShapeDtypeStruct; vm=pl.BlockSpec(memory_space=pltpu.VMEM)
+    return pl.pallas_call(unpack_kernel,in_specs=[vm]*2,out_specs=[vm]*5,
         out_shape=[S(logits.shape,f32)]+[S((RANK,wide),f32)]*3+[S((RANK,HD),f32)],
-        scratch_shapes=[pltpu.SemaphoreType.DMA((5,))],
         compiler_params=pltpu.CompilerParams(vmem_limit_bytes=60*2**20))(logits,grads)
 
-UNITS=8
-FIRST={-1: [0], 0: [1], 1: [2], 2: [3], 3: [4], 4: [5], 5: [6], 6: [7]}
-LATE=1
-PLAN={(1, 0): [(0, 1)], (2, 0): [(1, 1), (0, 2)], (2, 1): [], (3, 0): [(2, 1), (1, 2), (0, 3)], (4, 0): [(3, 1), (2, 2), (1, 3), (0, 4)], (5, 0): [(3, 2), (2, 3), (1, 4), (0, 5)], (6, 0): [(3, 3), (2, 4), (1, 5)], (7, 0): [(3, 4), (2, 5)], (7, 1): [(3, 5)]}
+UNIT=[(0,0,64),(0,64,64),(1,0,128),(2,0,128),(3,0,128),(4,0,128),(5,0,128),(6,0,128),(7,0,128)]
+ROUND=[(0,0,128),(0,128,272),(1,0,272),(2,0,272),(3,0,272)]
+UNITS=len(UNIT); RN=len(ROUND)
+FIRST={-1:[0],0:[1],1:[2],2:[3],3:[4],4:[5],5:[6],6:[7],7:[8]}
+PLAN={(1, 0): [(0, 1)], (2, 0): [(0, 2), (1, 1)], (3, 0): [(0, 3), (1, 2), (2, 1)], (4, 0): [(0, 4), (1, 3), (2, 2), (3, 1)], (5, 0): [(0, 5), (1, 4), (2, 3), (3, 2), (4, 1)], (6, 0): [(1, 5), (2, 4), (3, 3), (4, 2)], (7, 0): [(2, 5), (3, 4), (4, 3)], (8, 0): [(3, 5), (4, 4)], (8, 1): [(4, 5)]}
 
 def gather_kernel(mem_ref, slab_ref, wq_ref, wk_ref, wv_ref, qdown_hbm, vdown_hbm, qup_hbm, vup_hbm, ret_hbm,
                   pool, q_out, k_out, v_out, low_out, asked_out,
@@ -344,8 +347,9 @@
     devc=(tm(x,z,1-c),y)
     devy=[(t,lax.rem(y+1,Y)),(t,lax.rem(y+Y-1,Y))]
     def rows_of(u):
-        return (mem_ref if u<MB else slab_ref).at[pl.ds((u%MB)*BLK,BLK)]
-    own=lambda u: pltpu.make_async_copy(rows_of(u),feat.at[u,y],osem.at[u])
+        fb,r0,n=UNIT[u]
+        return (mem_ref if fb<MB else slab_ref).at[pl.ds(fb%MB*BLK+r0,n)]
+    own=lambda fb: pltpu.make_async_copy((mem_ref if fb<MB else slab_ref).at[pl.ds(fb%MB*BLK,BLK)],feat.at[fb,y],osem.at[fb])
     loads=[pltpu.make_async_copy(a,b,lsem.at[i]) for i,(a,b) in enumerate([(wk_ref,wkv.at[:,0:HD]),(wv_ref,wkv.at[:,HD:2*HD]),(vdown_hbm,vdown_ref),(vup_hbm,vup_ref),(ret_hbm,ret_ref),(wq_ref,wq),(qdown_hbm,qdown_ref),(qup_hbm,qup_ref)])]
     bar=pltpu.get_barrier_semaphore()
     for dev in devx[1:]+devz+devy+[devc]:
@@ -356,24 +360,30 @@
     def rc(src,dst,s,r,dev):
         return pltpu.make_async_remote_copy(src_ref=src,dst_ref=dst,send_sem=s,recv_sem=r,device_id=dev,device_id_type=MESH)
     left=lax.rem(y+Y-1,Y); right=lax.rem(y+1,Y)
-    H=BLK//2
-    def y_first(u): return [rc(rows_of(u),feat.at[u,y],ysem.at[0,u,i],ysem.at[1,u,i],devy[i]) for i in range(2)]
-    def y_pass(u): return [rc(feat.at[u,left,pl.ds(0,H)],feat.at[u,left,pl.ds(0,H)],ysem.at[0,u,2],ysem.at[1,u,2],devy[0]),
-                           rc(feat.at[u,right,pl.ds(H,H)],feat.at[u,right,pl.ds(H,H)],ysem.at[0,u,3],ysem.at[1,u,3],devy[1])]
+    def piece_of(u,h,half=None):
+        fb,r0,n=UNIT[u]
+        return feat.at[fb,h,pl.ds(r0,n) if half is None else pl.ds(r0+half*(n//2),n//2)]
+    def y_first(u): return [rc(rows_of(u),piece_of(u,y),ysem.at[0,u,i],ysem.at[1,u,i],devy[i]) for i in range(2)]
+    def y_pass(u): return [rc(piece_of(u,h,i),piece_of(u,h,i),ysem.at[0,u,2+i],ysem.at[1,u,2+i],devy[i]) for i,h in enumerate((left,right))]
     def start(cs):
         for cp in cs: cp.start()
     asked=lambda k: rc(mine,asked_out.at[k],xsem.at[0,k],xsem.at[1,k],devx[k])
 
-    def part(b,cc,xs,zs): return pool.at[b,cc,xs,zs]
+    def part(r,cc,xs,zs):
+        b,lo,hi=ROUND[r]
+        return pool.at[b,cc,xs,zs,pl.ds(lo,hi-lo)]
+    def fresh(r):
+        b,lo,hi=ROUND[r]
+        return stage.at[b,pl.ds(lo,hi-lo)]
     every=pl.ds(0,X)
     GROUP=[pl.ds(0,1),pl.ds(1,2),pl.ds(3,2),pl.ds(5,2),pl.ds(7,1)]
     def share(b,cc,g): return rc(part(b,cc,every,GROUP[g]),part(b,cc,every,GROUP[g]),ssem.at[b,32+g],rsem.at[b,32+g],devc)
-    def keep(b): return pltpu.make_async_copy(stage.at[b],pool.at[b,c,x,0],psem.at[b])
-    def x_own(b,k): return rc(stage.at[b],pool.at[b,0,x,0],ssem.at[b,k-1],rsem.at[b,k],devx[k])
+    def keep(b): return pltpu.make_async_copy(fresh(b),part(b,c,x,0),psem.at[b])
+    def x_own(b,k): return rc(fresh(b),part(b,0,x,0),ssem.at[b,k-1],rsem.at[b,k],devx[k])
     back=[x]+[lax.rem(x+X-k,X) for k in range(1,X)]
     def hop0(b,l,i,k):
         src=part(b,0,back[k],0 if l==0 else 2*l-1+i)
-        return rc(stage.at[b] if l==0 and k==0 else src,part(b,0,back[k],2*l+1+i),ssem.at[b,3+8*l+2*k+i],rsem.at[b,4+8*l+2*k+i],devz[i])
+        return rc(fresh(b) if l==0 and k==0 else src,part(b,0,back[k],2*l+1+i),ssem.at[b,3+8*l+2*k+i],rsem.at[b,4+8*l+2*k+i],devz[i])
     def last0(b,k):
         low=back[k]<X//2
         dev=(jnp.where(low,devz[0][0],devz[1][0]),y)
@@ -395,11 +405,11 @@
             for k in range(X): last0(b,k).wait_recv()
         share(b,0,phase-1).start()
     def hop1(b,l,i):
-        src=stage.at[b] if l==0 else pool.at[b,1,x,2*l-1+i]
-        return rc(src,pool.at[b,1,x,2*l+1+i if l<3 else 7],ssem.at[b,3+2*l+i if l<3 else 9],rsem.at[b,4+2*l+i if l<3 else 10],devz[i])
+        src=fresh(b) if l==0 else part(b,1,x,2*l-1+i)
+        return rc(src,part(b,1,x,2*l+1+i if l<3 else 7),ssem.at[b,3+2*l+i if l<3 else 9],rsem.at[b,4+2*l+i if l<3 else 10],devz[i])
     def spread(b,g,k):
-        src=part(b,1,x,GROUP[g])
-        return rc(stage.at[pl.ds(b,1)] if g==0 else src,src,ssem.at[b,12+5*(k-1)+g],rsem.at[b,12+5*(k-1)+g],devx[k])
+        src=part(b,1,x,0 if g==0 else GROUP[g])
+        return rc(fresh(b) if g==0 else src,src,ssem.at[b,12+5*(k-1)+g],rsem.at[b,12+5*(k-1)+g],devx[k])
     def pass_on(b,g):
         for k in range(1,X): spread(b,g,k).wait_recv()
         share(b,1,g).start()
@@ -432,18 +442,19 @@
         pl.when(c==1)(lambda: core1(b,phase))
 
     def project(u):
-        own(u).wait()
+        fb,r0,n=UNIT[u]
+        if r0==0: own(fb).wait()
         if u==0:
             for i in range(4): loads[i].wait()
-        if u==MB:
+        memory=fb<MB
+        if fb==MB:
             for i in range(5,8): loads[i].wait()
-        memory=u<MB
-        pair=jnp.zeros((BLK,2*HD),f32)
-        low=jnp.zeros((RANK if memory else 2*RANK,BLK),f32)
+        pair=jnp.zeros((n,2*HD),f32)
+        low=jnp.zeros((RANK if memory else 2*RANK,n),f32)
         wide=wq.shape[1]
         for h in range(Y):
             cols=slice(h*wide,(h+1)*wide)
-            piece=feat[u,h]
+            piece=feat[fb,h,r0:r0+n]
             pair=pair+jnp.dot(piece,wkv[cols,:],preferred_element_type=f32)
             down=vdown_ref[:,cols] if memory else jnp.concatenate([qdown_ref[:,cols],vdown_ref[:,cols]],axis=0)
             low=low+lax.dot_general(down,piece,NT,preferred_element_type=f32)
@@ -451,22 +462,23 @@
         keys=pair[:,:HD].astype(bf16)
         values=(pair[:,HD:]+lax.dot_general(low[-RANK:],vup_ref[...],TN,preferred_element_type=f32)).astype(bf16)
         if memory:
-            stage[u,0:BLK,:]=keys
-            stage[u,BLK:2*BLK,:]=values
-            stage[u,2*BLK:,:]=low
+            for i in range(0,n,64):
+                stage[fb,2*(r0+i):2*(r0+i)+64,:]=keys[i:i+64]
+                stage[fb,2*(r0+i)+64:2*(r0+i)+128,:]=values[i:i+64]
+            stage[fb,2*BLK:,r0:r0+n]=low
         else:
-            b=u-MB
+            b=fb-MB
             rows=slice(b*BLK,(b+1)*BLK)
             k_out[rows,:]=keys
             v_out[rows,:]=values
             low_out[:,rows]=low
             acc=lax.dot_general(low[:RANK],qup_ref[...],TN,preferred_element_type=f32)
             for h in range(Y):
-                acc=acc+jnp.dot(feat[u,h],wq[h*wide:(h+1)*wide,:],preferred_element_type=f32)
+                acc=acc+jnp.dot(feat[fb,h],wq[h*wide:(h+1)*wide,:],preferred_element_type=f32)
             q_out[rows,:]=acc.astype(bf16)
 
     for v in FIRST[-1]: start(y_first(v))
-    for u in range(UNITS): own(u).start()
+    for fb in range(2*MB): own(fb).start()
     for cp in loads[4:]: cp.start()
     mine[...]=jnp.full(mine.shape,-1,jnp.int32)
     loads[4].wait()
@@ -477,17 +489,18 @@
         for cp in y_first(u): cp.wait_recv()
         start(y_pass(u))
         for v in FIRST.get(u,[]): start(y_first(v))
-        if LATE and u>MB: project(u-1)
+        if u>RN: project(u-1)
         for b,p in PLAN.get((u,0),[]): step(b,p)
         for cp in y_pass(u): cp.wait_recv()
-        if u<MB or not LATE: project(u)
-        if u<MB: begin(u)
+        if u<RN:
+            project(u)
+            begin(u)
         for b,p in PLAN.get((u,1),[]): step(b,p)
-    if LATE: project(UNITS-1)
+    project(UNITS-1)
     for k in range(1,X): asked(k).wait()
     for u in range(UNITS):
         for cp in y_first(u)+y_pass(u): cp.wait_send()
-    for b in range(MB):
+    for b in range(RN):
         for g in range(5):
             share(b,1-c,g).wait_recv()
             share(b,c,g).wait_send()
@@ -514,9 +527,9 @@
         in_specs=[hbm]*10,
         out_specs=[hbm]+[vm]*5,
         out_shape=[S((MB,2,X,Z,ROWS,HD),bf16),S((n,wide),bf16),S((n,HD),bf16),S((n,HD),bf16),S((2*RANK,n),bf16),S((X,8,128),jnp.int32)],
-        scratch_shapes=[V((UNITS,Y,BLK,wide),bf16),V(wq.shape,bf16),V((wq.shape[0],2*HD),bf16),V(qdown.shape,bf16),V(vdown.shape,bf16),V(qup.shape,bf16),V(vup.shape,bf16),V(ret.shape,jnp.int32),
+        scratch_shapes=[V((2*MB,Y,BLK,wide),bf16),V(wq.shape,bf16),V((wq.shape[0],2*HD),bf16),V(qdown.shape,bf16),V(vdown.shape,bf16),V(qup.shape,bf16),V(vup.shape,bf16),V(ret.shape,jnp.int32),
             V((MB,ROWS,HD),bf16),V((8,128),jnp.int32),
-            D((2,UNITS,4)),D((MB,37)),D((MB,37)),D((8,)),D((MB,)),D((UNITS,)),D((2,X))],
+            D((2,UNITS,4)),D((RN,37)),D((RN,37)),D((8,)),D((RN,)),D((2*MB,)),D((2,X))],
         compiler_params=pltpu.CompilerParams(collective_id=2,has_side_effects=True,vmem_limit_bytes=60*2**20),
     )(mem,slab,wq,wk,wv,qdown,vdown,qup,vup,ret)
 

time: 158 us -> 151 us (0.956)
  Pallas kernels: 157 us -> 150 us
    pallas_call x1, Pallas kernels: 7.11 us -> 1.61 us  [unpack(): pl.pallas_call(unpack_kernel, in_specs=[vm] * 2, out_specs=[vm] * 5, out_...]
    pallas_call x1, Pallas kernels: 93.2 us -> 91.2 us  [gather_all(): pl.pallas_call(gather_kernel, in_specs=[hbm] * 10, out_specs=[hbm] + [vm]...]
where the time goes in v5:
time: 151 us
  Pallas kernels  150 us (99%)
    pallas_call x1, Pallas kernels, gather_all(): pl.pallas_call(gather_kernel, in_specs=[hbm] * 10, out_specs=[hbm] + [vm]...  91.2 us
    pallas_call x1, Pallas kernels, reduce_all(): pl.pallas_call(reduce_kernel, in_specs=[pl.BlockSpec(memory_space=pl.ANY)...  36.1 us
    pallas_call x1, Pallas kernels, attend(): pl.pallas_call(attend_kernel, grid_spec=pltpu.PrefetchScalarGridSpec(num_...  21.4 us

profile of v5, /device:TPU:1, one launch (start us, length us, event | category | flops | bytes accessed | tf_op | source)
XLA Modules:
  0.0 151.1 jit_solution(17709665705448781544)
XLA Ops:
  0.6 91.2 %shard_map.164 = (bf16[4,2,4,8,272,128]{5,4,3,2,1,0:T(8,128)(2,1)}, bf16[512,896]{1,0:T(8,128)(2,1)}, bf16[512,128]{1,0:T(8,128)(2,1)}, bf16[512,128]{1,0:T(8,12...) custom-call(bf16[512,896]{1,0:T(8,128)(2,1)} %mem_hbm.1, bf16[512,896]{1,0:T(8,128)(2,1)} %slab_hbm.1, ...), custom_call_target="tpu_custom_call" | custom-call | tf_op jit(solution)/shard_map/pallas_call | solution.py:526
  91.9 21.4 %shard_map.165 = (f32[4,40,128]{2,1,0:T(8,128)}, f32[16,896]{1,0:T(8,128)}, f32[16,128]{1,0:T(8,128)}, bf16[64,16,128]{2,1,0:T(8,128)(2,1)}) custom-call(s32[4,8]{1,0:T(4,128)} %ret.1, s32[4]{0:T(128)} %bnd.1, bf16[512,896]{1,0:T(8,128)(2,1)} %get-tuple-element.23.q_hbm, bf16[512,128]{1,0:T(8,128)(2,1)} %get-tuple-element.24.kl_hbm, ...), custom_call_target="tpu_custom_call" | custom-call | tf_op jit(solution)/shard_map/pallas_call | solution.py:144
  113.3 36.1 %shard_map.166 = (f32[8,512]{1,0:T(8,128)}, f32[16,2816]{1,0:T(8,128)}) custom-call(s32[4,8,128]{2,1,0:T(8,128)} %get-tuple-element.22.asked_hbm, f32[4,40,128]{2,1,0:T(8,128)} %get-tuple-element.28.cols_hbm, f32[16,896]{1,0:T(8,128)} %get-tuple-element.29.qug_hbm, f32[16,128]{1,0:T(8,128)} %get-tuple-element.30.vug_hbm, ...), custom_call_target="tpu_custom_call" | custom-call | tf_op jit(solution)/shard_map/pallas_call | solution.py:306
  149.4 1.6 %shard_map.167 = (f32[8,512]{1,0:T(8,128)}, f32[16,896]{1,0:T(8,128)}, f32[16,896]{1,0:T(8,128)}, f32[16,896]{1,0:T(8,128)}, f32[16,128]{1,0:T(8,128)}) custom-call(f32[8,512]{1,0:T(8,128)} %get-tuple-element.32.logits, f32[16,2816]{1,0:T(8,128)} %get-tuple-element.33.grads), custom_call_target="tpu_custom_call" | custom-call | tf_op jit(solution)/shard_map/pallas_call | solution.py:328

commit v6 on v5

--- a/solution.py
+++ b/solution.py
@@ -28,10 +28,8 @@
     loads=[pltpu.make_async_copy(src,dst,lsem.at[i]) for i,(src,dst) in enumerate([(q_hbm,q_ref),(kl_hbm,kl_ref),(vl_hbm,vl_ref),(low_hbm,low_ref),(gt_hbm,gt_ref),(twt_hbm,twt_ref),(qup_hbm,qup_ref),(vup_hbm,vup_ref)])]
     @pl.when(c==0)
     def _():
+        for i in range(TOP): fetch(i).start()
         for cp in loads: cp.start()
-        def go(i,_):
-            fetch(i).start(); return 0
-        lax.fori_loop(0,4*TOP,go,0)
         qug_ref[...]=jnp.zeros_like(qug_ref)
         vug_ref[...]=jnp.zeros_like(vug_ref)
         mc[...]=jnp.zeros_like(mc)
@@ -59,6 +57,9 @@
             kk[dst,:]=land[i,half*128:half*128+64,:]
             vv[dst,:]=land[i,half*128+64:half*128+128,:]
         lt[:,s*BLK:(s+1)*BLK]=land[i,256:272,:]
+    @pl.when(c<pl.num_programs(0)-1)
+    def _():
+        for s in range(TOP): fetch((c+1)*TOP+s).start()
     own=slice(TOP*BLK,nkeys)
     kk[own,:]=kl_ref[rows,:]
     vv[own,:]=vl_ref[rows,:]
@@ -331,13 +332,13 @@
 
 UNIT=[(0,0,64),(0,64,64),(1,0,128),(2,0,128),(3,0,128),(4,0,128),(5,0,128),(6,0,128),(7,0,128)]
 ROUND=[(0,0,128),(0,128,272),(1,0,272),(2,0,272),(3,0,272)]
-UNITS=len(UNIT); RN=len(ROUND)
+UNITS=len(UNIT); RN=len(ROUND); DONE=3
 FIRST={-1:[0],0:[1],1:[2],2:[3],3:[4],4:[5],5:[6],6:[7],7:[8]}
 PLAN={(1, 0): [(0, 1)], (2, 0): [(0, 2), (1, 1)], (3, 0): [(0, 3), (1, 2), (2, 1)], (4, 0): [(0, 4), (1, 3), (2, 2), (3, 1)], (5, 0): [(0, 5), (1, 4), (2, 3), (3, 2), (4, 1)], (6, 0): [(1, 5), (2, 4), (3, 3), (4, 2)], (7, 0): [(2, 5), (3, 4), (4, 3)], (8, 0): [(3, 5), (4, 4)], (8, 1): [(4, 5)]}
 
 def gather_kernel(mem_ref, slab_ref, wq_ref, wk_ref, wv_ref, qdown_hbm, vdown_hbm, qup_hbm, vup_hbm, ret_hbm,
-                  pool, q_out, k_out, v_out, low_out, asked_out,
-                  feat, wq, wkv, qdown_ref, vdown_ref, qup_ref, vup_ref, ret_ref, stage, mine, ysem, ssem, rsem, lsem, psem, osem, xsem):
+                  pool, q_hbm, k_hbm, v_hbm, low_hbm, asked_out,
+                  q_out, k_out, v_out, low_out, feat, wq, wkv, qdown_ref, vdown_ref, qup_ref, vup_ref, ret_ref, stage, mine, ysem, ssem, rsem, lsem, psem, osem, xsem, wsem):
     t=lax.axis_index("tm"); y=lax.axis_index("heads")
     x=lax.div(t,ZC); z=lax.rem(lax.div(t,2),Z); c=lax.rem(t,2)
     def tm(xx,zz,cc): return (xx*Z+zz)*2+cc
@@ -441,6 +442,10 @@
         pl.when(c==0)(lambda: core0(b,phase))
         pl.when(c==1)(lambda: core1(b,phase))
 
+    def leave(b):
+        rows=pl.ds(b*BLK,BLK)
+        jobs=[(q_out.at[rows],q_hbm.at[rows]),(k_out.at[rows],k_hbm.at[rows]),(v_out.at[rows],v_hbm.at[rows]),(low_out.at[:,rows],low_hbm.at[:,rows])]
+        return [pltpu.make_async_copy(src,dst,wsem.at[b,i]) for i,(src,dst) in enumerate(jobs)]
     def project(u):
         fb,r0,n=UNIT[u]
         if r0==0: own(fb).wait()
@@ -476,34 +481,14 @@
             for h in range(Y):
                 acc=acc+jnp.dot(feat[fb,h],wq[h*wide:(h+1)*wide,:],preferred_element_type=f32)
             q_out[rows,:]=acc.astype(bf16)
-
-    for v in FIRST[-1]: start(y_first(v))
-    for fb in range(2*MB): own(fb).start()
-    for cp in loads[4:]: cp.start()
-    mine[...]=jnp.full(mine.shape,-1,jnp.int32)
-    loads[4].wait()
-    mine[0:MB,0:TOP]=ret_ref[...]
-    for k in range(1,X): asked(k).start()
-    asked_out[0]=mine[...]
-    for u in range(UNITS):
-        for cp in y_first(u): cp.wait_recv()
-        start(y_pass(u))
-        for v in FIRST.get(u,[]): start(y_first(v))
-        if u>RN: project(u-1)
-        for b,p in PLAN.get((u,0),[]): step(b,p)
-        for cp in y_pass(u): cp.wait_recv()
-        if u<RN:
-            project(u)
-            begin(u)
-        for b,p in PLAN.get((u,1),[]): step(b,p)
-    project(UNITS-1)
-    for k in range(1,X): asked(k).wait()
-    for u in range(UNITS):
-        for cp in y_first(u)+y_pass(u): cp.wait_send()
-    for b in range(RN):
+            for cp in leave(b): cp.start()
+
+    def over(b):
         for g in range(5):
             share(b,1-c,g).wait_recv()
             share(b,c,g).wait_send()
+        keepers(b)
+    def keepers(b):
         @pl.when(c==0)
         def _():
             for k in range(1,X): x_own(b,k).wait_send()
@@ -518,6 +503,37 @@
             hop1(b,3,b%2).wait_send()
             for g in range(5):
                 for k in range(1,X): spread(b,g,k).wait_send()
+    def settled(u):
+        for cp in y_first(u)+y_pass(u): cp.wait_send()
+
+    for v in FIRST[-1]: start(y_first(v))
+    for fb in range(2*MB): own(fb).start()
+    for cp in loads[4:]: cp.start()
+    mine[...]=jnp.full(mine.shape,-1,jnp.int32)
+    loads[4].wait()
+    mine[0:MB,0:TOP]=ret_ref[...]
+    for k in range(1,X): asked(k).start()
+    asked_out[0]=mine[...]
+    for u in range(UNITS):
+        for cp in y_first(u): cp.wait_recv()
+        start(y_pass(u))
+        for v in FIRST.get(u,[]): start(y_first(v))
+        if u>RN: project(u-1)
+        if u>=2: settled(u-2)
+        if u==3:
+            for k in range(1,X): asked(k).wait()
+        if 0<=u-RN-1<DONE: over(u-RN-1)
+        for b,p in PLAN.get((u,0),[]): step(b,p)
+        for cp in y_pass(u): cp.wait_recv()
+        if u<RN:
+            project(u)
+            begin(u)
+        elif u==UNITS-1: project(u)
+        for b,p in PLAN.get((u,1),[]): step(b,p)
+    for u in range(UNITS-2,UNITS): settled(u)
+    for b in range(DONE,RN): over(b)
+    for b in range(MB):
+        for cp in leave(b): cp.wait()
 
 def gather_all(mem,slab,wq,wk,wv,qdown,vdown,qup,vup,ret):
     vm=pl.BlockSpec(memory_space=pltpu.VMEM); hbm=pl.BlockSpec(memory_space=pl.ANY)
@@ -525,11 +541,11 @@
     S=jax.ShapeDtypeStruct; V=pltpu.VMEM; D=pltpu.SemaphoreType.DMA
     return pl.pallas_call(gather_kernel,
         in_specs=[hbm]*10,
-        out_specs=[hbm]+[vm]*5,
+        out_specs=[hbm]*5+[vm],
         out_shape=[S((MB,2,X,Z,ROWS,HD),bf16),S((n,wide),bf16),S((n,HD),bf16),S((n,HD),bf16),S((2*RANK,n),bf16),S((X,8,128),jnp.int32)],
-        scratch_shapes=[V((2*MB,Y,BLK,wide),bf16),V(wq.shape,bf16),V((wq.shape[0],2*HD),bf16),V(qdown.shape,bf16),V(vdown.shape,bf16),V(qup.shape,bf16),V(vup.shape,bf16),V(ret.shape,jnp.int32),
+        scratch_shapes=[V((n,wide),bf16),V((n,HD),bf16),V((n,HD),bf16),V((2*RANK,n),bf16),V((2*MB,Y,BLK,wide),bf16),V(wq.shape,bf16),V((wq.shape[0],2*HD),bf16),V(qdown.shape,bf16),V(vdown.shape,bf16),V(qup.shape,bf16),V(vup.shape,bf16),V(ret.shape,jnp.int32),
             V((MB,ROWS,HD),bf16),V((8,128),jnp.int32),
-            D((2,UNITS,4)),D((RN,37)),D((RN,37)),D((8,)),D((RN,)),D((2*MB,)),D((2,X))],
+            D((2,UNITS,4)),D((RN,37)),D((RN,37)),D((8,)),D((RN,)),D((2*MB,)),D((2,X)),D((MB,4))],
         compiler_params=pltpu.CompilerParams(collective_id=2,has_side_effects=True,vmem_limit_bytes=60*2**20),
     )(mem,slab,wq,wk,wv,qdown,vdown,qup,vup,ret)
 

time: 151 us -> 151 us (level)
  no operation moved by 1% of the time
where the time goes in v6:
time: 151 us; the launch traced here: 150 us
  Pallas kernels  150 us (99%)
    pallas_call x1, Pallas kernels, gather_all(): pl.pallas_call(gather_kernel, in_specs=[hbm] * 10, out_specs=[hbm] * 5 +...  90.9 us
    pallas_call x1, Pallas kernels, reduce_all(): pl.pallas_call(reduce_kernel, in_specs=[pl.BlockSpec(memory_space=pl.ANY)...  35.2 us
    pallas_call x1, Pallas kernels, attend(): pl.pallas_call(attend_kernel, grid_spec=pltpu.PrefetchScalarGridSpec(num_...  22 us

profile of v6, /device:TPU:1, one launch (start us, length us, event | category | flops | bytes accessed | tf_op | source)
XLA Modules:
  0.0 150.4 jit_solution(5771475320761826159)
XLA Ops:
  0.6 90.9 %shard_map.164 = (bf16[4,2,4,8,272,128]{5,4,3,2,1,0:T(8,128)(2,1)}, bf16[512,896]{1,0:T(8,128)(2,1)}, bf16[512,128]{1,0:T(8,128)(2,1)}, bf16[512,128]{1,0:T(8,12...) custom-call(bf16[512,896]{1,0:T(8,128)(2,1)} %mem_hbm.1, bf16[512,896]{1,0:T(8,128)(2,1)} %slab_hbm.1, ...), custom_call_target="tpu_custom_call" | custom-call | tf_op jit(solution)/shard_map/pallas_call | solution.py:542
  91.6 22.0 %shard_map.165 = (f32[4,40,128]{2,1,0:T(8,128)}, f32[16,896]{1,0:T(8,128)}, f32[16,128]{1,0:T(8,128)}, bf16[64,16,128]{2,1,0:T(8,128)(2,1)}) custom-call(s32[4,8]{1,0:T(4,128)} %ret.1, s32[4]{0:T(128)} %bnd.1, bf16[512,896]{1,0:T(8,128)(2,1)} %get-tuple-element.23.q_hbm, bf16[512,128]{1,0:T(8,128)(2,1)} %get-tuple-element.24.kl_hbm, ...), custom_call_target="tpu_custom_call" | custom-call | tf_op jit(solution)/shard_map/pallas_call | solution.py:145
  113.6 35.2 %shard_map.166 = (f32[8,512]{1,0:T(8,128)}, f32[16,2816]{1,0:T(8,128)}) custom-call(s32[4,8,128]{2,1,0:T(8,128)} %get-tuple-element.22.asked_hbm, f32[4,40,128]{2,1,0:T(8,128)} %get-tuple-element.28.cols_hbm, f32[16,896]{1,0:T(8,128)} %get-tuple-element.29.qug_hbm, f32[16,128]{1,0:T(8,128)} %get-tuple-element.30.vug_hbm, ...), custom_call_target="tpu_custom_call" | custom-call | tf_op jit(solution)/shard_map/pallas_call | solution.py:307
  148.8 1.6 %shard_map.167 = (f32[8,512]{1,0:T(8,128)}, f32[16,896]{1,0:T(8,128)}, f32[16,896]{1,0:T(8,128)}, f32[16,896]{1,0:T(8,128)}, f32[16,128]{1,0:T(8,128)}) custom-call(f32[8,512]{1,0:T(8,128)} %get-tuple-element.32.logits, f32[16,2816]{1,0:T(8,128)} %get-tuple-element.33.grads), custom_call_target="tpu_custom_call" | custom-call | tf_op jit(solution)/shard_map/pallas_call | solution.py:329

commit v7 on v6

--- a/solution.py
+++ b/solution.py
@@ -28,8 +28,10 @@
     loads=[pltpu.make_async_copy(src,dst,lsem.at[i]) for i,(src,dst) in enumerate([(q_hbm,q_ref),(kl_hbm,kl_ref),(vl_hbm,vl_ref),(low_hbm,low_ref),(gt_hbm,gt_ref),(twt_hbm,twt_ref),(qup_hbm,qup_ref),(vup_hbm,vup_ref)])]
     @pl.when(c==0)
     def _():
-        for i in range(TOP): fetch(i).start()
         for cp in loads: cp.start()
+        def go(i,_):
+            fetch(i).start(); return 0
+        lax.fori_loop(0,4*TOP,go,0)
         qug_ref[...]=jnp.zeros_like(qug_ref)
         vug_ref[...]=jnp.zeros_like(vug_ref)
         mc[...]=jnp.zeros_like(mc)
@@ -57,9 +59,6 @@
             kk[dst,:]=land[i,half*128:half*128+64,:]
             vv[dst,:]=land[i,half*128+64:half*128+128,:]
         lt[:,s*BLK:(s+1)*BLK]=land[i,256:272,:]
-    @pl.when(c<pl.num_programs(0)-1)
-    def _():
-        for s in range(TOP): fetch((c+1)*TOP+s).start()
     own=slice(TOP*BLK,nkeys)
     kk[own,:]=kl_ref[rows,:]
     vv[own,:]=vl_ref[rows,:]
@@ -125,14 +124,16 @@
     high=whole.astype(bf16)
     rest=(whole-high.astype(f32)).astype(bf16)
     up=vup_ref[...]
-    cot=lax.dot_general(up,high,NT,preferred_element_type=f32)+lax.dot_general(up,rest,NT,preferred_element_type=f32)
+    both=jnp.concatenate([high,rest],axis=1)
+    cot=lax.dot_general(jnp.concatenate([up,up],axis=1),both,NT,preferred_element_type=f32)
     cols_ref[c,TAGS+RANK:,:]=cot[:,own]
     for s in range(TOP):
         o=lax.div(ret[c,s],MB)
         zo=lax.rem(lax.div(o,2),Z)
         mc[lax.div(o,ZC)*ZC+lax.rem(zo,Y)*4+lax.div(zo,Y)*2+lax.rem(o,2)]+=cot[:,s*BLK:(s+1)*BLK]
     side=lt[...]
-    vug_ref[...]+=jnp.dot(side,high,preferred_element_type=f32)+jnp.dot(side,rest,preferred_element_type=f32)
+    sums=jnp.dot(side,both,preferred_element_type=f32)
+    vug_ref[...]+=sums[:,:HD]+sums[:,HD:]
     @pl.when(c==pl.num_programs(0)-1)
     def _():
         mcot_ref[...]=mc[...].astype(bf16)

time: 151 us -> 150 us (level)
  no operation moved by 1% of the time
where the time goes in v7:
time: 150 us
  Pallas kernels  149 us (99%)
    pallas_call x1, Pallas kernels, gather_all(): pl.pallas_call(gather_kernel, in_specs=[hbm] * 10, out_specs=[hbm] * 5 +...  90.9 us
    pallas_call x1, Pallas kernels, reduce_all(): pl.pallas_call(reduce_kernel, in_specs=[pl.BlockSpec(memory_space=pl.ANY)...  35.3 us
    pallas_call x1, Pallas kernels, attend(): pl.pallas_call(attend_kernel, grid_spec=pltpu.PrefetchScalarGridSpec(num_...  21.7 us

profile of v7, /device:TPU:1, one launch (start us, length us, event | category | flops | bytes accessed | tf_op | source)
XLA Modules:
  0.0 150.1 jit_solution(4448663054636496574)
XLA Ops:
  0.6 90.9 %shard_map.164 = (bf16[4,2,4,8,272,128]{5,4,3,2,1,0:T(8,128)(2,1)}, bf16[512,896]{1,0:T(8,128)(2,1)}, bf16[512,128]{1,0:T(8,128)(2,1)}, bf16[512,128]{1,0:T(8,12...) custom-call(bf16[512,896]{1,0:T(8,128)(2,1)} %mem_hbm.1, bf16[512,896]{1,0:T(8,128)(2,1)} %slab_hbm.1, ...), custom_call_target="tpu_custom_call" | custom-call | tf_op jit(solution)/shard_map/pallas_call | solution.py:543
  91.6 21.7 %shard_map.165 = (f32[4,40,128]{2,1,0:T(8,128)}, f32[16,896]{1,0:T(8,128)}, f32[16,128]{1,0:T(8,128)}, bf16[64,16,128]{2,1,0:T(8,128)(2,1)}) custom-call(s32[4,8]{1,0:T(4,128)} %ret.1, s32[4]{0:T(128)} %bnd.1, bf16[512,896]{1,0:T(8,128)(2,1)} %get-tuple-element.23.q_hbm, bf16[512,128]{1,0:T(8,128)(2,1)} %get-tuple-element.24.kl_hbm, ...), custom_call_target="tpu_custom_call" | custom-call | tf_op jit(solution)/shard_map/pallas_call | solution.py:146
  113.3 35.3 %shard_map.166 = (f32[8,512]{1,0:T(8,128)}, f32[16,2816]{1,0:T(8,128)}) custom-call(s32[4,8,128]{2,1,0:T(8,128)} %get-tuple-element.22.asked_hbm, f32[4,40,128]{2,1,0:T(8,128)} %get-tuple-element.28.cols_hbm, f32[16,896]{1,0:T(8,128)} %get-tuple-element.29.qug_hbm, f32[16,128]{1,0:T(8,128)} %get-tuple-element.30.vug_hbm, ...), custom_call_target="tpu_custom_call" | custom-call | tf_op jit(solution)/shard_map/pallas_call | solution.py:308
  148.5 1.6 %shard_map.167 = (f32[8,512]{1,0:T(8,128)}, f32[16,896]{1,0:T(8,128)}, f32[16,896]{1,0:T(8,128)}, f32[16,896]{1,0:T(8,128)}, f32[16,128]{1,0:T(8,128)}) custom-call(f32[8,512]{1,0:T(8,128)} %get-tuple-element.32.logits, f32[16,2816]{1,0:T(8,128)} %get-tuple-element.33.grads), custom_call_target="tpu_custom_call" | custom-call | tf_op jit(solution)/shard_map/pallas_call | solution.py:330
